TPU v7x, 32 devices: a whole 2x2x4 slice. The times are simulated.
32 devices in a mesh: branch: 2 (over x), series: 16 (over z, y, core).
Axes of the slice: x: 2, y: 2, z: 4, core: 2. Of those that a mesh axis runs over, the one named last changes fastest.
Arguments:
- series_in: bfloat16 [16, 816, 512], P('series'), may hold values from -6 to 6
- target: bfloat16 [16, 816, 512], P('series', 'branch'), may hold values from -6 to 6
- horizons: int32 [16], P('series'), may hold values from 96 to 720, as said below
- observed: int32 [16, 816], P('series'), may hold values 0 or 1
- down_short: bfloat16 [6144, 512], P('series'), may hold values from -0.078125 to 0.078125
- iso_short: bfloat16 [35328, 512], P('series'), may hold values from -0.046875 to 0.046875
- trans_short: bfloat16 [6144, 512], P('series'), may hold values from -0.25 to 0.25
- down_long: bfloat16 [8192, 512], P('series'), may hold values from -0.0625 to 0.0625
- iso_long: bfloat16 [26624, 512], P('series'), may hold values from -0.0546875 to 0.0546875
- trans_long: bfloat16 [8192, 512], P('series'), may hold values from -0.25 to 0.25
- branch_bias: float32 [2, 4, 512], P('branch'), may hold values from -2 to 2
- branch_gain: float32 [2, 512], P('branch'), may hold values from 0.5 to 1.5
- merge_weight: bfloat16 [2, 512, 512], replicated, may hold values from -0.1875 to 0.1875
- head_bias: float32 [4, 512], replicated, may hold values from -2 to 2
- head_gain: float32 [2, 512], replicated, may hold values from 0.5 to 1.5
- ff_in: bfloat16 [512, 2048], replicated, may hold values from -0.25 to 0.25
- ff_in_bias: float32 [2048], replicated, may hold values from -2 to 2
- ff_out: bfloat16 [2048, 512], replicated, may hold values from -0.125 to 0.125
Outputs:
- out: bfloat16 [16, 816, 512], P('series', 'branch')
- series_loss: float32 [16], P('series')
- grad_input: float32 [16, 816, 512], P('series')
- grad_down_short: float32 [6144, 512], P('series')
- grad_iso_short: float32 [35328, 512], P('series')
- grad_trans_short: float32 [6144, 512], P('series')
- grad_down_long: float32 [8192, 512], P('series')
- grad_iso_long: float32 [26624, 512], P('series')
- grad_trans_long: float32 [8192, 512], P('series')
- grad_branch_bias: float32 [2, 4, 512], replicated
- grad_branch_gain: float32 [2, 512], replicated
- grad_merge: float32 [2, 512, 512], replicated
- grad_head_bias: float32 [4, 512], replicated
- grad_head_gain: float32 [2, 512], replicated
- grad_ff_in: float32 [512, 2048], P(None, 'series')
- grad_ff_in_bias: float32 [2048], replicated
- grad_ff_out: float32 [2048, 512], P('series')
Inputs may be any that keep to these rules, and one draw needn't show every extreme that they name: `horizons`: each horizon is one of 96, 192, 336 and 720; the shortest and the longest occur in every draw.
All inputs are finite; a program needn't handle non-finite values. No bound on the sum of `observed` on one device may be relied on, other than what follows from the above.
Results may differ from a plain program's by a relative error of at most 0.018.
Values may be sent and summed in bfloat16 or wider, within the bound.
No kernel may reach another device: no remote copies, remote signals or barrier semaphores. Data moves between devices by JAX's collectives and lax.ppermute only.
A program may use at most 448 MiB of HBM per device.

v0:
```python
import jax
import jax.numpy as jnp
from jax import lax
from jax.sharding import PartitionSpec as P

SCALE_S = 12
SCALE_L = 16
SEQ_IN = 96


EPSILON = 1e-05


def layer_norm(values, gain_row, shift_row):
    center = values - jnp.mean(values, axis=-1, keepdims=True)
    spread = jnp.mean(center * center, axis=-1, keepdims=True)
    return center * lax.rsqrt(spread + EPSILON) * gain_row + shift_row


def gelu_exact(values):
    return jax.nn.gelu(values, approximate=False)


def product(first_operand, second_operand):
    return jnp.dot(first_operand, second_operand, preferred_element_type=jnp.float32)


def left_product(first_operand, second_operand):
    return jnp.einsum(
        "mi,mo->io", first_operand, second_operand, preferred_element_type=jnp.float32
    )


def right_product(first_operand, second_operand):
    return jnp.einsum(
        "mo,io->mi", first_operand, second_operand, preferred_element_type=jnp.float32
    )


def fitted(matrix, row_total):
    return jnp.pad(matrix, ((0, row_total - matrix.shape[0]), (0, 0)))


def unpack(gathered_all, shards, rows_max, rows_own):
    features = gathered_all.shape[1]
    return gathered_all.reshape(shards, rows_max, features)[:, :rows_own].reshape(
        shards * rows_own, features
    )


def repack(gradient, shards, rows_max):
    rows_own = gradient.shape[0] // shards
    shaped = gradient.reshape(shards, rows_own, gradient.shape[1])
    return jnp.pad(shaped, ((0, 0), (0, rows_max - rows_own), (0, 0))).reshape(
        shards * rows_max, gradient.shape[1]
    )


def branch_pass(series_in, weights, shards, rows_max, biases, gain_row, factor):
    series_count, length, features = series_in.shape
    step_count = (length + factor) // factor
    margin = factor // 2
    weight_down = unpack(weights[0], shards, rows_max[0], factor * features // shards)
    weight_iso = unpack(weights[1], shards, rows_max[1], step_count * features // shards)
    weight_trans = unpack(weights[2], shards, rows_max[2], factor * features // shards).reshape(
        factor, features, features
    )
    blocks = jnp.pad(series_in, ((0, 0), (margin, step_count * factor - length - margin), (0, 0)))
    blocks = blocks.reshape(series_count * step_count, factor * features)
    act_down = jnp.tanh(product(blocks, weight_down) + biases[0])
    low_down = act_down.astype(jnp.bfloat16)
    padded = jnp.concatenate(
        [
            jnp.zeros((series_count, step_count - 1, features), jnp.bfloat16),
            low_down.reshape(series_count, step_count, features),
        ],
        axis=1,
    )
    unfolded = jnp.concatenate(
        [padded[:, offset : offset + step_count] for offset in range(step_count)], axis=2
    )
    unfolded = unfolded.reshape(series_count * step_count, step_count * features)
    act_iso = jnp.tanh(product(unfolded, weight_iso) + biases[1])
    inner_norm, inner_back = jax.vjp(
        layer_norm, act_iso + low_down.astype(jnp.float32), gain_row, biases[3]
    )
    low_inner = inner_norm.astype(jnp.bfloat16)
    spread_out = jnp.einsum(
        "mi,jio->mjo", low_inner, weight_trans, preferred_element_type=jnp.float32
    )
    act_trans = jnp.tanh(
        spread_out.reshape(series_count, step_count * factor, features)[:, :length] + biases[2]
    )
    result, outer_back = jax.vjp(
        layer_norm, act_trans + series_in.astype(jnp.float32), gain_row, biases[3]
    )
    stored = (
        blocks,
        weight_down,
        weight_iso,
        weight_trans,
        act_down,
        unfolded,
        act_iso,
        inner_back,
        low_inner,
        act_trans,
        outer_back,
    )
    return (result, stored)


def branch_back(series_in, weights, shards, rows_max, biases, gain_row, factor, upstream):
    series_count, length, features = series_in.shape
    step_count = (length + factor) // factor
    margin = factor // 2
    result, stored = branch_pass(series_in, weights, shards, rows_max, biases, gain_row, factor)
    (
        blocks,
        weight_down,
        weight_iso,
        weight_trans,
        act_down,
        unfolded,
        act_iso,
        inner_back,
        low_inner,
        act_trans,
        outer_back,
    ) = stored
    delta_outer, gain_outer, shift_outer = outer_back(upstream)
    delta_trans = (delta_outer * (1.0 - act_trans * act_trans)).astype(jnp.bfloat16)
    trans_blocks = jnp.pad(delta_trans, ((0, 0), (0, step_count * factor - length), (0, 0)))
    trans_blocks = trans_blocks.reshape(series_count * step_count, factor, features)
    grad_trans = jnp.einsum(
        "mi,mjo->jio", low_inner, trans_blocks, preferred_element_type=jnp.float32
    )
    grad_trans = grad_trans.reshape(factor * features, features)
    inner_upstream = jnp.einsum(
        "mjo,jio->mi", trans_blocks, weight_trans, preferred_element_type=jnp.float32
    )
    delta_inner, gain_inner, shift_inner = inner_back(inner_upstream)
    delta_iso = (delta_inner * (1.0 - act_iso * act_iso)).astype(jnp.bfloat16)
    grad_iso = left_product(unfolded, delta_iso)
    delta_unfold = right_product(delta_iso, weight_iso).reshape(
        series_count, step_count, step_count, features
    )
    delta_padded = jnp.zeros((series_count, 2 * step_count - 1, features), jnp.float32)
    for offset in range(step_count):
        delta_padded = delta_padded.at[:, offset : offset + step_count].add(
            delta_unfold[:, :, offset]
        )
    delta_low = (
        delta_padded[:, step_count - 1 :].reshape(series_count * step_count, features) + delta_inner
    )
    delta_down = (delta_low * (1.0 - act_down * act_down)).astype(jnp.bfloat16)
    grad_down = left_product(blocks, delta_down)
    delta_blocks = right_product(delta_down, weight_down).reshape(
        series_count, step_count * factor, features
    )
    delta_series = delta_blocks[:, margin : margin + length] + delta_outer
    vectors = jnp.stack(
        [
            jnp.sum(delta_down.astype(jnp.float32), axis=0),
            jnp.sum(delta_iso.astype(jnp.float32), axis=0),
            jnp.sum(delta_trans.astype(jnp.float32), axis=(0, 1)),
            shift_inner + shift_outer,
        ]
    )
    padded_grads = (
        repack(grad_down, shards, rows_max[0]),
        repack(grad_iso, shards, rows_max[1]),
        repack(grad_trans, shards, rows_max[2]),
    )
    return (delta_series, padded_grads, vectors, gain_inner + gain_outer)


def body(
    series_in,
    target,
    horizons,
    observed,
    down_short,
    iso_short,
    trans_short,
    down_long,
    iso_long,
    trans_long,
    branch_bias,
    branch_gain,
    merge_weight,
    head_bias,
    head_gain,
    ff_in,
    ff_in_bias,
    ff_out,
):
    branch_index = lax.axis_index("branch")
    shards = lax.axis_size("series")
    series_count, length, features = series_in.shape
    rows_max = (
        max(down_short.shape[0], down_long.shape[0]),
        max(iso_short.shape[0], iso_long.shape[0]),
        max(trans_short.shape[0], trans_long.shape[0]),
    )
    is_short = branch_index == 0
    own_down = jnp.where(is_short, fitted(down_short, rows_max[0]), fitted(down_long, rows_max[0]))
    own_iso = jnp.where(is_short, fitted(iso_short, rows_max[1]), fitted(iso_long, rows_max[1]))
    own_trans = jnp.where(
        is_short, fitted(trans_short, rows_max[2]), fitted(trans_long, rows_max[2])
    )
    gathered = (
        lax.all_gather(own_down, "series", axis=0, tiled=True),
        lax.all_gather(own_iso, "series", axis=0, tiled=True),
        lax.all_gather(own_trans, "series", axis=0, tiled=True),
    )
    biases = branch_bias[0]
    gain_row = branch_gain[0]

    def forward_with(factor):
        return lambda: branch_pass(series_in, gathered, shards, rows_max, biases, gain_row, factor)[
            0
        ].astype(jnp.bfloat16)

    branch_out = lax.cond(is_short, forward_with(SCALE_S), forward_with(SCALE_L))
    received = lax.all_to_all(
        branch_out.reshape(series_count, length, 1, features),
        "branch",
        split_axis=1,
        concat_axis=2,
        tiled=True,
    )
    half_rows = received.shape[1]
    merge_rows = received.reshape(series_count * half_rows, 2 * features)
    merge_flat = merge_weight.reshape(2 * features, features)
    merged = product(merge_rows, merge_flat) + head_bias[0]
    normed, first_back = jax.vjp(layer_norm, merged, head_gain[0], head_bias[2])
    low_normed = normed.astype(jnp.bfloat16)
    pre_ff = product(low_normed, ff_in) + ff_in_bias
    activated, gelu_back = jax.vjp(gelu_exact, pre_ff)
    low_act = activated.astype(jnp.bfloat16)
    ff_result = product(low_act, ff_out) + head_bias[1]
    final_out, second_back = jax.vjp(layer_norm, merged + ff_result, head_gain[1], head_bias[3])
    final_rows = final_out.reshape(series_count, half_rows, features)
    positions = branch_index * half_rows + jnp.arange(half_rows, dtype=jnp.int32)
    observed_half = lax.dynamic_slice_in_dim(observed, branch_index * half_rows, half_rows, 1)
    valid_mask = (
        observed_half.astype(jnp.float32)
        * (positions >= SEQ_IN).astype(jnp.float32)
        * (positions < SEQ_IN + horizons[:, None]).astype(jnp.float32)
    )
    error_rows = final_rows - target.astype(jnp.float32)
    weighted = valid_mask[:, :, None] * error_rows
    series_part = 0.5 * jnp.sum(weighted * error_rows, axis=(1, 2)) / (features * length)
    delta_sum, gain_second, shift_second = second_back(
        weighted.reshape(series_count * half_rows, features)
    )
    delta_ff = delta_sum.astype(jnp.bfloat16)
    grad_ff_out = left_product(low_act, delta_ff)
    delta_act = right_product(delta_ff, ff_out)
    (delta_pre,) = gelu_back(delta_act)
    low_pre = delta_pre.astype(jnp.bfloat16)
    grad_ff_in = left_product(low_normed, low_pre)
    delta_normed = right_product(low_pre, ff_in)
    delta_first, gain_first, shift_first = first_back(delta_normed)
    delta_merged = (delta_first + delta_sum).astype(jnp.bfloat16)
    grad_merge = left_product(merge_rows, delta_merged).reshape(2, features, features)
    delta_rows = (
        right_product(delta_merged, merge_flat)
        .astype(jnp.bfloat16)
        .reshape(series_count, half_rows, 2, features)
    )
    back_rows = lax.all_to_all(delta_rows, "branch", split_axis=2, concat_axis=1, tiled=True)
    upstream = back_rows.astype(jnp.float32).reshape(series_count, length, features)
    ff_shares = (
        lax.psum_scatter(grad_ff_in, "series", scatter_dimension=1, tiled=True),
        lax.psum_scatter(grad_ff_out, "series", scatter_dimension=0, tiled=True),
    )
    weights_back = (
        lax.all_gather(own_down, "series", axis=0, tiled=True),
        lax.all_gather(own_iso, "series", axis=0, tiled=True),
        lax.all_gather(own_trans, "series", axis=0, tiled=True),
    )

    def backward_with(factor):
        return lambda: branch_back(
            series_in, weights_back, shards, rows_max, biases, gain_row, factor, upstream
        )

    delta_series, padded_grads, vectors, gain_grad = lax.cond(
        is_short, backward_with(SCALE_S), backward_with(SCALE_L)
    )
    reduced = (
        lax.psum_scatter(padded_grads[0], "series", scatter_dimension=0, tiled=True),
        lax.psum_scatter(padded_grads[1], "series", scatter_dimension=0, tiled=True),
        lax.psum_scatter(padded_grads[2], "series", scatter_dimension=0, tiled=True),
    )
    short_flag = is_short.astype(jnp.float32)
    long_flag = 1.0 - short_flag
    summed = (
        lax.psum(delta_series.astype(jnp.bfloat16), "branch").astype(jnp.float32),
        lax.psum(series_part.astype(jnp.bfloat16), "branch").astype(jnp.float32),
        lax.psum(
            (short_flag * reduced[0][: down_short.shape[0]]).astype(jnp.bfloat16), "branch"
        ).astype(jnp.float32),
        lax.psum((short_flag * reduced[1]).astype(jnp.bfloat16), "branch").astype(jnp.float32),
        lax.psum(
            (short_flag * reduced[2][: trans_short.shape[0]]).astype(jnp.bfloat16), "branch"
        ).astype(jnp.float32),
        lax.psum((long_flag * reduced[0]).astype(jnp.bfloat16), "branch").astype(jnp.float32),
        lax.psum(
            (long_flag * reduced[1][: iso_long.shape[0]]).astype(jnp.bfloat16), "branch"
        ).astype(jnp.float32),
        lax.psum((long_flag * reduced[2]).astype(jnp.bfloat16), "branch").astype(jnp.float32),
        lax.psum(ff_shares[0].astype(jnp.bfloat16), "branch").astype(jnp.float32),
        lax.psum(ff_shares[1].astype(jnp.bfloat16), "branch").astype(jnp.float32),
    )
    selector = (jnp.arange(2, dtype=jnp.int32) == branch_index).astype(jnp.float32)
    full_bias = selector[:, None, None] * vectors[None]
    full_gain = selector[:, None] * gain_grad[None]
    head_vectors = jnp.stack(
        [
            jnp.sum(delta_merged.astype(jnp.float32), axis=0),
            jnp.sum(delta_ff.astype(jnp.float32), axis=0),
            shift_first,
            shift_second,
        ]
    )
    head_gains = jnp.stack([gain_first, gain_second])
    ff_bias_grad = jnp.sum(low_pre.astype(jnp.float32), axis=0)
    totals = lax.psum(
        (grad_merge, head_vectors, head_gains, ff_bias_grad, full_bias, full_gain),
        ("branch", "series"),
    )
    return (
        final_rows.astype(jnp.bfloat16),
        summed[1],
        summed[0],
        summed[2],
        summed[3],
        summed[4],
        summed[5],
        summed[6],
        summed[7],
        totals[4],
        totals[5],
        totals[0],
        totals[1],
        totals[2],
        summed[8],
        totals[3],
        summed[9],
    )


def solution(mesh):
    placed = (
        P("series", None, None),
        P("series", "branch", None),
        P("series"),
        P("series", None),
        P("series", None),
        P("series", None),
        P("series", None),
        P("series", None),
        P("series", None),
        P("series", None),
        P("branch", None, None),
        P("branch", None),
        P(),
        P(),
        P(),
        P(),
        P(),
        P(),
    )
    return jax.shard_map(
        body,
        mesh=mesh,
        in_specs=placed,
        out_specs=(
            P("series", "branch", None),
            P("series"),
            P("series", None, None),
            P("series", None),
            P("series", None),
            P("series", None),
            P("series", None),
            P("series", None),
            P("series", None),
            P(),
            P(),
            P(),
            P(),
            P(),
            P(None, "series"),
            P(),
            P("series", None),
        ),
        check_vma=False,
    )
```

profile of v0, /device:TPU:0, one launch (start us, length us, event | category | flops | bytes accessed | tf_op | source)
XLA Modules:
  0.0 2365.2 jit_solution(14898251557672402315)
XLA Ops:
  16.4 72.0 %all-gather.4.cloned.1.call-done = bf16[8192,512]{1,0:T(8,128)(2,1)} async-done(((bf16[512,512]{1,0:T(8,128)(2,1)}), bf16[8192,512]{1,0:T(8,128)(2,1)}) %all-gather.4.cloned.1.call-update) | async-done | bytes 8388624 | tf_op jit(solution)/shard_map/all_gather | solution.py:213
  88.4 75.9 %all-gather.8.cloned.1.call-done = bf16[8192,512]{1,0:T(8,128)(2,1)} async-done(((bf16[512,512]{1,0:T(8,128)(2,1)}), bf16[8192,512]{1,0:T(8,128)(2,1)}) %all-gather.8.cloned.1.call-update) | async-done | bytes 8388624 | tf_op jit(solution)/shard_map/all_gather | solution.py:215
  164.3 180.9 %all-gather.6.cloned.1.call-done = bf16[35328,512]{1,0:T(8,128)(2,1)} async-done(((bf16[2208,512]{1,0:T(8,128)(2,1)}), bf16[35328,512]{1,0:T(8,128)(2,1)}) %all-gather.6.cloned.1.call-update) | async-done | bytes 36175888 | tf_op jit(solution)/shard_map/all_gather | solution.py:214
  345.2 90.3 %conditional.6 = (bf16[1,816,512]{2,1,0:T(8,128)(2,1)}) conditional(s32[]{:T(128)} %convert_element_type.273, (bf16[1,816,512]{2,1,0:T(8,128)(2,1)S(1)}, bf16[8192,512]{1,0:T(8,128)(2,1)}, f32[4,512]{1,0:T(4,128)S(1)}, bf16[35328,512]{1,0:T(8,128)(2,1)}, f32[1,512]{1,0:T(1,128)S(1)}, /*index=5*/bf16[8192,512]{1,0:T(8,128)(2,1)}) %tuple.692, ...), branch_computations={%region_0.5_spmd, %region_5.10_spmd} | conditional | flops 3372371968 | bytes 125288984
  404.8 16.2 fusion.195
  453.7 12.0 all-to-all-done
  504.2 13.5 all_to_all.24
  518.0 476.9 %conditional.7 = (f32[8192,512]{1,0:T(8,128)}, f32[35328,512]{1,0:T(8,128)}, f32[4,512]{1,0:T(4,128)S(1)}, f32[1,816,512]{2,1,0:T(8,128)}, f32[1,816,512]{2,1,0:...) conditional(s32[]{:T(128)} %convert_element_type.273, ...), branch_computations={%region_20.35_spmd.clone, %region_35.50_spmd.clone} | conditional | flops 10111068160 | bytes 538687360 | solution.py:290
  587.2 16.9 fusion.188
  628.3 20.6 fusion.208
  648.9 11.9 reshape.4517
  662.2 9.0 fusion.200
  703.2 11.0 fusion.199
  774.6 10.9 fusion.198
  785.5 10.9 fusion.197
  934.4 13.0 pad.312
  953.8 13.0 pad.311
  966.8 27.9 %fusion.126 = f32[35328,512]{1,0:T(8,128)} fusion(bf16[69,512]{1,0:T(8,128)(2,1)S(1)} %copy-done.29, bf16[1,69,35328]{2,1,0:T(8,128)(2,1)} %constant_dynamic-update-slice_fusion.173), kind=kOutput, calls=%fused_computation.553 | convolution fusion | flops 2496135168 | bytes 77297664 | tf_op jit(solution)/shard_map/cond/branch_1_fun/mi,mo->io/dot_general | solution.py:29
  1002.9 170.0 %reduce-scatter.6.cloned.1.call-done = f32[512,512]{1,0:T(8,128)} async-done(((f32[8192,512]{1,0:T(8,128)}), f32[512,512]{1,0:T(8,128)}) %reduce-scatter.6.cloned.1.call-update) | async-done | bytes 1048592 | tf_op jit(solution)/shard_map/reduce_scatter | solution.py:294
  1174.9 179.8 %reduce-scatter.10.cloned.1.call-done = f32[512,512]{1,0:T(8,128)} async-done(((f32[8192,512]{1,0:T(8,128)}), f32[512,512]{1,0:T(8,128)}) %reduce-scatter.10.cloned.1.call-update) | async-done | bytes 1048592 | tf_op jit(solution)/shard_map/reduce_scatter | solution.py:296
  1359.7 677.6 %reduce-scatter.8.cloned.1.call-done = f32[2208,512]{1,0:T(8,128)} async-done(((f32[35328,512]{1,0:T(8,128)}), f32[2208,512]{1,0:T(8,128)}) %reduce-scatter.8.cloned.1.call-update) | async-done | bytes 4522000 | tf_op jit(solution)/shard_map/reduce_scatter | solution.py:295
  2058.0 40.9 %all-reduce.18 = (f32[2,4,512]{2,1,0:T(4,128)}, f32[2,512]{1,0:T(2,128)}, f32[4,512]{1,0:T(4,128)}, f32[2,512]{1,0:T(2,128)}, f32[2048]{0:T(1024)}) all-reduce(f32[2,4,512]{2,1,0:T(4,128)S(1)} %broadcast_multiply_fusion.8, f32[2,512]{1,0:T(2,128)S(1)} %broadcast_multiply_fusion.9, ...), channel_id=1, replica_groups=mesh['branch'=2,'series'=16] {'branch','series'}, use_global_device_ids=true, to_apply=%region_60.61 | all-reduce | flops 10240 | bytes 81920 | tf_op jit(solution)/shard_map/psum | solution.py:331
  2098.9 114.2 %all-reduce.25.cloned.1.call-done = (bf16[1,816,512]{2,1,0:T(8,128)(2,1)}, bf16[384,512]{1,0:T(8,128)(2,1)}, bf16[2208,512]{1,0:T(8,128)(2,1)}, bf16[384,512]{1,...) async-done(((bf16[1,816,512]{2,1,0:T(8,128)(2,1)}, ...) | async-done | bytes 6897680 | tf_op jit(solution)/shard_map/psum | solution.py:301
  2229.2 124.7 %all-reduce.23.cloned.1.call-done = f32[2,512,512]{2,1,0:T(8,128)} async-done(((f32[2,512,512]{2,1,0:T(8,128)}), f32[2,512,512]{2,1,0:T(8,128)}) %all-reduce.23.cloned.1.call-update) | async-done | bytes 2097168 | tf_op jit(solution)/shard_map/psum | solution.py:331
  (533 shorter events, 513.7 us)
Async XLA Ops:
  7.2 464.9 %copy-start = (bf16[512,2048]{1,0:T(8,128)(2,1)S(1)}, bf16[512,2048]{1,0:T(8,128)(2,1)}, u32[]{:S(2)}) copy-start(bf16[512,2048]{1,0:T(8,128)(2,1)} %param.279) | copy-start | bytes 6291460
  7.2 81.2 %all-gather.4.cloned.1.call-start = ((), (), s32[]{:S(2)}) async-start(), calls=%async_computation.7 | async-start | bytes 8912896 | tf_op jit(solution)/shard_map/all_gather | solution.py:213
  9.3 155.0 %all-gather.8.cloned.1.call-start = ((), (), s32[]{:S(2)}) async-start(), calls=%async_computation.9 | async-start | bytes 8912896 | tf_op jit(solution)/shard_map/all_gather | solution.py:215
  11.3 333.8 %copy-start.2 = (bf16[1,816,512]{2,1,0:T(8,128)(2,1)S(1)}, bf16[1,816,512]{2,1,0:T(8,128)(2,1)}, u32[]{:S(2)}) copy-start(bf16[1,816,512]{2,1,0:T(8,128)(2,1)} %param.264) | copy-start | bytes 2506756
  11.4 333.8 %copy-start.30 = (f32[1,512]{1,0:T(1,128)S(1)}, f32[1,512]{1,0:T(1,128)}, u32[]{:S(2)}) copy-start(f32[1,512]{1,0:T(1,128)} %param.275) | copy-start | bytes 6148
  11.4 333.8 %copy-start.34 = (f32[1,4,512]{2,1,0:T(4,128)S(1)}, f32[1,4,512]{2,1,0:T(4,128)}, u32[]{:S(2)}) copy-start(f32[1,4,512]{2,1,0:T(4,128)} %param.274) | copy-start | bytes 24580
  11.4 333.8 %all-gather.6.cloned.1.call-start = ((), (), s32[]{:S(2)}) async-start(), calls=%async_computation.8 | async-start | bytes 38436864 | tf_op jit(solution)/shard_map/all_gather | solution.py:214
  16.4 466.0 %copy-start.37 = (f32[1,408]{1,0:T(1,128)}, f32[1,408]{1,0:T(1,128)S(1)}, u32[]{:S(2)}) copy-start(f32[1,408]{1,0:T(1,128)S(1)} %compare_select_fusion.1) | copy-start | bytes 4900
  439.1 14.6 copy-start.50
  439.1 14.6 copy-start.49
  449.3 16.4 all-to-all-start
  453.6 546.0 %reduce-scatter.12.cloned.1.call-start = ((), (), s32[]{:S(2)}) async-start(), calls=%async_computation.14 | async-start | bytes 4456448 | tf_op jit(solution)/shard_map/reduce_scatter | solution.py:276
  453.7 28.7 %copy-start.39 = (f32[1,512]{1,0:T(1,128)}, f32[1,512]{1,0:T(1,128)S(1)}, u32[]{:S(2)}) copy-start(f32[1,512]{1,0:T(1,128)S(1)} %get-tuple-element.1892) | copy-start | bytes 6148
  453.7 28.7 %copy-start.43 = (f32[1,512]{1,0:T(1,128)}, f32[1,512]{1,0:T(1,128)S(1)}, u32[]{:S(2)}) copy-start(f32[1,512]{1,0:T(1,128)S(1)} %get-tuple-element.1888) | copy-start | bytes 6148
  471.8 16.4 copy-start.21
  492.9 508.3 %reduce-scatter.14.cloned.1.call-start = ((), (), s32[]{:S(2)}) async-start(), calls=%async_computation.15 | async-start | bytes 4456448 | tf_op jit(solution)/shard_map/reduce_scatter | solution.py:277
  497.8 675.1 %reduce-scatter.6.cloned.1.call-start = ((), (), s32[]{:S(2)}) async-start(), calls=%async_computation.10 | async-start | bytes 17825792 | tf_op jit(solution)/shard_map/reduce_scatter | solution.py:294
  628.1 20.8 copy-start.26
  628.3 20.6 copy-start.28
  994.9 359.7 %reduce-scatter.10.cloned.1.call-start = ((), (), s32[]{:S(2)}) async-start(), calls=%async_computation.12 | async-start | bytes 17825792 | tf_op jit(solution)/shard_map/reduce_scatter | solution.py:296
  995.7 1041.7 %reduce-scatter.8.cloned.1.call-start = ((), (), s32[]{:S(2)}) async-start(), calls=%async_computation.11 | async-start | bytes 76873728 | tf_op jit(solution)/shard_map/reduce_scatter | solution.py:295
  996.4 1216.6 %all-reduce.25.cloned.1.call-start = ((), (), s32[]{:S(2)}) async-start(), calls=%async_computation.16 | async-start | bytes 13795328 | tf_op jit(solution)/shard_map/psum | solution.py:301
  2043.3 310.6 %all-reduce.23.cloned.1.call-start = ((), (), s32[]{:S(2)}) async-start(), calls=%async_computation.13 | async-start | bytes 4194304 | tf_op jit(solution)/shard_map/psum | solution.py:331
  2226.4 130.5 %copy-start.1 = (bf16[512,2048]{1,0:T(8,128)(2,1)S(1)}, bf16[512,2048]{1,0:T(8,128)(2,1)}, u32[]{:S(2)}) copy-start(bf16[512,2048]{1,0:T(8,128)(2,1)} %param.279) | copy-start | bytes 6291460
  (43 other events, 227.9 us)
Sparse Core Ops, SparseCore 0:
  10.8 77.5 all-gather.3
  91.1 73.1 all-gather.7
  166.5 178.6 all-gather.5
  493.0 71.6 reduce-scatter.11
  568.9 71.4 reduce-scatter.13
  995.1 177.7 reduce-scatter.5
  1177.0 177.6 reduce-scatter.9
  1359.0 678.3 reduce-scatter.7
  2043.3 169.6 all-reduce.24
  2219.7 134.1 all-reduce.22
where the time goes:
time: 2380 us; the launch traced here: 2370 us
  waiting for transfers between devices  1610 us (68%)
  local copies, waits for them, and re-layouts  342 us (14%)
  other arithmetic  176 us (7%)
  matrix products  145 us (6%)
  blocking collectives  60.6 us (3%)
    reduce_scatter x1, waiting for transfers between devices, body(): lax.psum_scatter(padded_grads[1], 'series', scatter_dimension=0, tiled=True)  678 us
    all_gather x1, waiting for transfers between devices, body(): lax.all_gather(own_iso, 'series', axis=0, tiled=True)  181 us
    reduce_scatter x1, waiting for transfers between devices, body(): lax.psum_scatter(padded_grads[2], 'series', scatter_dimension=0, tiled=True)  180 us
    reduce_scatter x1, waiting for transfers between devices, body(): lax.psum_scatter(padded_grads[0], 'series', scatter_dimension=0, tiled=True)  170 us
    psum x1, waiting for transfers between devices, body(): lax.psum((grad_merge, head_vectors, head_gains, ff_bias_grad, full_bias,...  125 us
    psum x1, waiting for transfers between devices, body(): lax.psum(delta_series.astype(jnp.bfloat16), 'branch').astype(jnp.float32)  114 us
    scatter-add x68, local copies, waits for them, and re-layouts, branch_back(): delta_padded.at[:, offset:offset + step_count]  106 us
    add x67, other arithmetic, branch_back(): delta_padded.at[:, offset:offset + step_count]  104 us
  transfers between devices with their start and end apart: 11, of which 9 were waited for; matrix products, arithmetic and copies ran while one was open for 22% of the time, Pallas kernels for 0%

commit v1 on v0

--- a/solution.py
+++ b/solution.py
@@ -1,14 +1,636 @@
+import functools
+
 import jax
 import jax.numpy as jnp
 from jax import lax
+from jax.experimental import pallas as pl
+from jax.experimental.pallas import tpu as pltpu
 from jax.sharding import PartitionSpec as P
 
 SCALE_S = 12
 SCALE_L = 16
 SEQ_IN = 96
-
-
 EPSILON = 1e-05
+LANE = 128
+
+BF = jnp.bfloat16
+F32 = jnp.float32
+
+
+def up8(count, base=8):
+    return -(-count // base) * base
+
+
+class Plan:
+    def __init__(self, shards, length, features, down_rows, iso_rows):
+        self.shards, self.length, self.features = shards, length, features
+        self.factors = (SCALE_S, SCALE_L)
+        self.steps = tuple((length + k) // k for k in self.factors)
+        self.rows = up8(max(self.steps))
+        self.down_rows = down_rows
+        self.iso_rows = iso_rows
+        self.down_max, self.iso_max = max(down_rows), max(iso_rows)
+        self.groups = tuple(r // LANE for r in down_rows)
+        self.pack = up8(max(g * n for g, n in zip(self.groups, self.steps)), 16)
+        self.taps = tuple(
+            max(-(-((d * r) % features + r) // features) for d in range(shards)) for r in iso_rows
+        )
+        self.taps_max = max(self.taps)
+        self.quarter = shards // 4
+        self.stage_rows = max(k * up8(n) for k, n in zip(self.factors, self.steps))
+
+    def mask(self, slot):
+        core, rest = divmod(slot, 2 * self.quarter)
+        side, line = divmod(rest, self.quarter)
+        return core | (side << 1) | (line << 2)
+
+
+def vmem(count):
+    return [pl.BlockSpec(memory_space=pltpu.VMEM) for _ in range(count)]
+
+
+SMEM = pl.BlockSpec(memory_space=pltpu.SMEM)
+ANY = pl.BlockSpec(memory_space=pl.ANY)
+
+
+def call(body, in_specs, outs, scratch, flops=0, moved=0, limit=56):
+    return pl.pallas_call(
+        body,
+        out_shape=[jax.ShapeDtypeStruct(s, d) for s, d in outs],
+        in_specs=in_specs,
+        out_specs=vmem(len(outs)),
+        scratch_shapes=scratch,
+        compiler_params=pltpu.CompilerParams(vmem_limit_bytes=limit << 20),
+        cost_estimate=pl.CostEstimate(flops=flops, bytes_accessed=moved, transcendentals=0),
+    )
+
+
+def dot(a, b, dims=((1,), (0,))):
+    return lax.dot_general(a, b, (dims, ((), ())), preferred_element_type=F32)
+
+
+def norm_parts(values):
+    center = values - jnp.mean(values, axis=-1, keepdims=True)
+    spread = jnp.mean(center * center, axis=-1, keepdims=True)
+    scale = lax.rsqrt(spread + EPSILON)
+    return center * scale, scale
+
+
+def norm_back(upstream, unit, scale, gain):
+    inner = upstream * gain
+    first = jnp.mean(inner, axis=-1, keepdims=True)
+    second = jnp.mean(inner * unit, axis=-1, keepdims=True)
+    return scale * (inner - first - unit * second)
+
+
+def keep_rows(values, count):
+    index = lax.broadcasted_iota(jnp.int32, values.shape, 0)
+    return jnp.where(index < count, values, 0.0)
+
+
+def both(meta, short, long):
+    pl.when(meta[0] == 0)(short)
+    pl.when(meta[0] == 1)(long)
+
+
+def split(rows, features):
+    return pltpu.VMEM((features // LANE, rows, LANE), F32)
+
+
+def put(ref, start, values, stride=1):
+    count = values.shape[0]
+    where = pl.ds(start, count) if stride == 1 else pl.ds(start, count, stride=stride)
+    for c in range(ref.shape[0]):
+        ref[c, where, :] = values[:, c * LANE : (c + 1) * LANE]
+
+
+def get(ref, start, count, stride=1):
+    where = pl.ds(start, count) if stride == 1 else pl.ds(start, count, stride=stride)
+    return jnp.concatenate([ref[c, where, :] for c in range(ref.shape[0])], axis=1)
+
+
+def prep_blocks(plan, meta, series):
+    length, features = plan.length, plan.features
+    per_tap = features // LANE
+    shape = (plan.shards, plan.pack, LANE)
+
+    def kernel(meta_ref, x_ref, out_ref, wide, packed):
+        def run(b):
+            k, n, groups = plan.factors[b], plan.steps[b], plan.groups[b]
+            margin = k // 2
+            wide[...] = jnp.zeros_like(wide)
+            put(wide, margin, x_ref[...].astype(F32))
+            packed[...] = jnp.zeros_like(packed)
+            for d in range(plan.shards):
+                for r in range(groups):
+                    j, c = divmod(d * groups + r, per_tap)
+                    packed[r * n : (r + 1) * n, :] = wide[c, pl.ds(j, n, stride=k), :]
+                out_ref[d] = packed[...].astype(BF)
+
+        both(meta_ref, lambda: run(0), lambda: run(1))
+
+    return call(
+        kernel,
+        [SMEM] + vmem(1),
+        [(shape, BF)],
+        [split(plan.stage_rows, features), pltpu.VMEM((plan.pack, LANE), F32)],
+        moved=2 * length * features * 2,
+        limit=16,
+    )(meta, series)[0]
+
+
+def down_partial(plan, meta, blocks, w_short, w_long):
+    shards, rows, features = plan.shards, plan.rows, plan.features
+    half = shards // 2
+    chunk = 4
+
+    def kernel(meta_ref, in_ref, ws_ref, wl_ref, keep_ref, send_ref, a_ref, wide, packed):
+        me = meta_ref[1]
+
+        def run(b, w_ref):
+            n, groups = plan.steps[b], plan.groups[b]
+            width = groups * LANE
+            wide[...] = jnp.zeros_like(wide)
+            for start in range(0, shards, chunk):
+                for i in range(chunk):
+                    packed[...] = in_ref[me ^ plan.mask(start + i)].astype(F32)
+                    for r in range(groups):
+                        wide[i * rows : i * rows + n, r * LANE : (r + 1) * LANE] = packed[
+                            r * n : (r + 1) * n, :
+                        ]
+                matrix = wide[...].astype(BF)
+                a_ref[start * rows : (start + chunk) * rows, :] = matrix
+                part = dot(matrix[:, :width], w_ref[...])
+                for i in range(chunk):
+                    slot = start + i
+                    piece = part[i * rows : (i + 1) * rows]
+                    if slot < half:
+                        keep_ref[slot] = piece
+                    else:
+                        send_ref[slot - half] = piece.astype(BF)
+
+        both(meta_ref, lambda: run(0, ws_ref), lambda: run(1, wl_ref))
+
+    return call(
+        kernel,
+        [SMEM] + vmem(3),
+        [
+            ((half, rows, features), F32),
+            ((half, rows, features), BF),
+            ((shards * rows, plan.down_max), BF),
+        ],
+        [
+            pltpu.VMEM((chunk * rows, plan.down_max), F32),
+            pltpu.VMEM((plan.pack, LANE), F32),
+        ],
+        flops=2 * shards * rows * features * plan.down_max,
+        moved=6 << 20,
+        limit=32,
+    )(meta, blocks, w_short, w_long)
+
+
+def low_rows(plan, meta, pieces, biases):
+    rows, features = plan.rows, plan.features
+
+    def kernel(meta_ref, *refs):
+        parts, bias_ref, low_ref, act_ref = refs[:-3], refs[-3], refs[-2], refs[-1]
+        total = parts[0][...]
+        for piece in parts[1:]:
+            total = total + piece[...].astype(F32)
+        act = keep_rows(jnp.tanh(total + bias_ref[0:1, :]), meta_ref[4])
+        act_ref[...] = act
+        low_ref[...] = act.astype(BF)
+
+    return call(
+        kernel,
+        [SMEM] + vmem(len(pieces) + 1),
+        [((rows, features), BF), ((rows, features), F32)],
+        [],
+        moved=1 << 19,
+        limit=16,
+    )(meta, *pieces, biases)
+
+
+def time_major(plan, slots, stage, target, lead, tail_from):
+    shards, rows = plan.shards, plan.rows
+    for q, slot in enumerate(slots):
+        put(stage, q, slot[...].astype(F32), shards)
+    body = shards * rows
+    if lead:
+        target[0 : lead * shards, :] = jnp.zeros((lead * shards, target.shape[1]), BF)
+    target[lead * shards : lead * shards + body, :] = get(stage, 0, body).astype(BF)
+    rest = target.shape[0] - lead * shards - body
+    if rest:
+        target[lead * shards + body :, :] = jnp.zeros((rest, target.shape[1]), BF)
+
+
+def slot_list(refs, plan):
+    singles = refs[:-1]
+    return list(singles) + [refs[-1].at[i] for i in range(plan.shards // 2)]
+
+
+def pad_weight(plan, b, meta_ref, w_ref, target):
+    target[...] = jnp.zeros_like(target)
+    shift = pl.multiple_of(meta_ref[3], 16)
+    target[pl.ds(shift, plan.iso_rows[b]), :] = w_ref[...]
+
+
+def iso_partial(plan, meta, slots, w_short, w_long, backward):
+    shards, rows, features = plan.shards, plan.rows, plan.features
+    half = shards // 2
+    steps_max = max(plan.steps)
+    extra = plan.taps_max + 2
+    buffer = (steps_max + rows + extra) * shards
+    count = len(slots)
+
+    def kernel(meta_ref, *refs):
+        slot_refs = slot_list(refs[:count], plan)
+        ws_ref, wl_ref, keep_ref, send_ref, stage, lined, padded = refs[count:]
+        first = meta_ref[2]
+
+        def run(b, w_ref):
+            n, taps = plan.steps[b], plan.taps[b]
+            pad_weight(plan, b, meta_ref, w_ref, padded)
+            if backward:
+                time_major(plan, slot_refs, stage, lined, extra, 0)
+            else:
+                time_major(plan, slot_refs, stage, lined, n - 1, 0)
+            for m in range(taps):
+                if backward:
+                    start = extra + n - 1 - first - m
+                else:
+                    start = first + m
+                start = pl.multiple_of(start * shards, 16)
+                window = lined[pl.ds(start, rows * shards), :]
+                weight = padded[m * features : (m + 1) * features, :]
+                part = dot(window, weight, ((1,), (1,)) if backward else ((1,), (0,)))
+                total = part if m == 0 else total + part
+            put(stage, 0, total)
+            for q in range(shards):
+                piece = get(stage, q, rows, shards)
+                if q < half:
+                    keep_ref[q] = piece
+                else:
+                    send_ref[q - half] = piece.astype(BF)
+
+        both(meta_ref, lambda: run(0, ws_ref), lambda: run(1, wl_ref))
+
+    return call(
+        kernel,
+        [SMEM] + vmem(count + 2),
+        [((half, rows, features), F32), ((half, rows, features), BF)],
+        [
+            split(rows * shards, features),
+            pltpu.VMEM((buffer, features), BF),
+            pltpu.VMEM((plan.taps_max * features, features), BF),
+        ],
+        flops=2 * shards * rows * features * features * plan.taps_max,
+        moved=10 << 20,
+        limit=40,
+    )(meta, *slots, w_short, w_long)
+
+
+def iso_weight(plan, meta, low_slots, delta_slots):
+    shards, rows, features = plan.shards, plan.rows, plan.features
+    steps_max = max(plan.steps)
+    extra = plan.taps_max + 2
+    buffer = (steps_max + rows + extra) * shards
+    count = len(low_slots)
+
+    def kernel(meta_ref, *refs):
+        low_refs = slot_list(refs[:count], plan)
+        delta_refs = slot_list(refs[count : 2 * count], plan)
+        grad_ref, sum_ref, stage, lined, delta, total, ordered = refs[2 * count :]
+        first = meta_ref[2]
+        me = meta_ref[1]
+        for q in range(shards):
+            ordered[pl.ds(me ^ plan.mask(q), 1), :] = jnp.sum(
+                delta_refs[q][...].astype(F32), axis=0, keepdims=True
+            )
+        sum_ref[...] = jnp.sum(ordered[...], axis=0, keepdims=True)
+        time_major(plan, delta_refs, stage, delta, 0, 0)
+
+        def run(b):
+            n, taps = plan.steps[b], plan.taps[b]
+            time_major(plan, low_refs, stage, lined, n - 1, 0)
+            for m in range(taps):
+                start = pl.multiple_of((first + m) * shards, 16)
+                window = lined[pl.ds(start, rows * shards), :]
+                total[m * features : (m + 1) * features, :] = dot(window, delta[...], ((0,), (0,)))
+            shift = pl.multiple_of(meta_ref[3], 16)
+            grad_ref[0 : plan.iso_rows[b], :] = total[pl.ds(shift, plan.iso_rows[b]), :].astype(BF)
+
+        both(meta_ref, lambda: run(0), lambda: run(1))
+
+    return call(
+        kernel,
+        [SMEM] + vmem(2 * count),
+        [((plan.iso_max, features), BF), ((1, features), F32)],
+        [
+            split(rows * shards, features),
+            pltpu.VMEM((buffer, features), BF),
+            pltpu.VMEM((rows * shards, features), BF),
+            pltpu.VMEM((plan.taps_max * features, features), F32),
+            pltpu.VMEM((shards, features), F32),
+        ],
+        flops=2 * shards * rows * features * features * plan.taps_max,
+        moved=10 << 20,
+        limit=48,
+    )(meta, *low_slots, *delta_slots)
+
+
+def fetch_weight(plan, b, source, target, sems):
+    own = plan.down_rows[b]
+    copies = [
+        pltpu.make_async_copy(
+            source.at[d, pl.ds(0, own)], target.at[pl.ds(d * own, own)], sems.at[d]
+        )
+        for d in range(plan.shards)
+    ]
+    for copy in copies:
+        copy.start()
+    return copies
+
+
+def branch_forward(plan, meta, pieces, low, series, trans, biases, gain):
+    rows, features, length = plan.rows, plan.features, plan.length
+    count = len(pieces)
+    half_rows = length // 2
+
+    def kernel(meta_ref, *refs):
+        parts = refs[:count]
+        (low_ref, x_ref, w_hbm, bias_ref, gain_ref) = refs[count : count + 5]
+        (keep_ref, send_ref, act_ref, inner_ref, iso_ref, weight, stage, sems) = refs[count + 5 :]
+
+        def run(b):
+            k, n = plan.factors[b], plan.steps[b]
+            copies = fetch_weight(plan, b, w_hbm, weight, sems)
+            pre = parts[0][...]
+            for piece in parts[1:]:
+                pre = pre + piece[...].astype(F32)
+            act_iso = jnp.tanh(pre + bias_ref[1:2, :])
+            iso_ref[...] = act_iso
+            unit, _ = norm_parts(act_iso + low_ref[...].astype(F32))
+            inner = keep_rows(unit * gain_ref[...] + bias_ref[3:4, :], n).astype(BF)
+            inner_ref[...] = inner
+            for copy in copies:
+                copy.wait()
+            fit = up8(n)
+            for j in range(k):
+                pre_trans = dot(inner, weight[j * features : (j + 1) * features, :])
+                put(stage, j, pre_trans[:fit], k)
+            act = jnp.tanh(get(stage, 0, length) + bias_ref[2:3, :])
+            act_ref[...] = act
+            unit_out, _ = norm_parts(act + x_ref[...].astype(F32))
+            put(stage, 0, unit_out * gain_ref[...] + bias_ref[3:4, :])
+            mine = pl.multiple_of(meta_ref[0] * half_rows, 8)
+            other = pl.multiple_of((1 - meta_ref[0]) * half_rows, 8)
+            keep_ref[...] = get(stage, mine, half_rows).astype(BF)
+            send_ref[...] = get(stage, other, half_rows).astype(BF)
+
+        both(meta_ref, lambda: run(0), lambda: run(1))
+
+    return call(
+        kernel,
+        [SMEM] + vmem(count + 2) + [ANY] + vmem(2),
+        [
+            ((half_rows, features), BF),
+            ((half_rows, features), BF),
+            ((length, features), F32),
+            ((rows, features), BF),
+            ((rows, features), F32),
+        ],
+        [
+            pltpu.VMEM((plan.shards * plan.down_max, features), BF),
+            split(plan.stage_rows, features),
+            pltpu.SemaphoreType.DMA((plan.shards,)),
+        ],
+        flops=2 * rows * features * features * SCALE_L,
+        moved=14 << 20,
+        limit=48,
+    )(meta, *pieces, low, series, trans, biases, gain)
+
+
+def branch_backward(plan, meta, up_keep, up_recv, series, act, act_iso, low, trans, biases, gain):
+    rows, features, length, shards = plan.rows, plan.features, plan.length, plan.shards
+    half_rows = length // 2
+
+    def kernel(
+        meta_ref, uk_ref, ur_ref, x_ref, act_ref, iso_ref, low_ref, w_hbm, bias_ref, gain_ref,
+        outer_ref, taps_ref, delta_iso_ref, delta_inner_ref, vec_ref, weight, stage, upstream, sems,
+    ):
+        def run(b):
+            k, n = plan.factors[b], plan.steps[b]
+            copies = fetch_weight(plan, b, w_hbm, weight, sems)
+            mine = pl.multiple_of(meta_ref[0] * half_rows, 8)
+            other = pl.multiple_of((1 - meta_ref[0]) * half_rows, 8)
+            upstream[pl.ds(mine, half_rows), :] = uk_ref[...].astype(F32)
+            upstream[pl.ds(other, half_rows), :] = ur_ref[...].astype(F32)
+            act_value = act_ref[...]
+            unit, scale = norm_parts(act_value + x_ref[...].astype(F32))
+            above = upstream[...]
+            vec_ref[...] = jnp.zeros_like(vec_ref)
+            shift_sum = jnp.sum(above, axis=0, keepdims=True)
+            gain_sum = jnp.sum(above * unit, axis=0, keepdims=True)
+            outer = norm_back(above, unit, scale, gain_ref[...])
+            outer_ref[...] = outer
+            delta = (outer * (1.0 - act_value * act_value)).astype(BF).astype(F32)
+            vec_ref[0:1, :] = jnp.sum(delta, axis=0, keepdims=True)
+            put(stage, 0, delta)
+            put(stage, length, jnp.zeros((plan.stage_rows - length, features), F32))
+            for copy in copies:
+                copy.wait()
+            fit = up8(n)
+            total = jnp.zeros((fit, features), F32)
+            pieces = []
+            for j in range(k):
+                piece = get(stage, j, fit, k).astype(BF)
+                total = total + dot(
+                    piece, weight[j * features : (j + 1) * features, :], ((1,), (1,))
+                )
+            own = plan.down_rows[b]
+            for d in range(shards):
+                tap = (2 * own * (d // 2)) // features + d % 2
+                piece = get(stage, tap, fit, k)
+                if fit < rows:
+                    piece = jnp.concatenate([piece, jnp.zeros((rows - fit, features), F32)], axis=0)
+                taps_ref[d] = piece.astype(BF)
+            if fit < rows:
+                total = jnp.concatenate([total, jnp.zeros((rows - fit, features), F32)], axis=0)
+            total = keep_rows(total, n)
+            act_in = iso_ref[...]
+            unit_in, scale_in = norm_parts(act_in + low_ref[...].astype(F32))
+            vec_ref[1:2, :] = shift_sum + jnp.sum(total, axis=0, keepdims=True)
+            vec_ref[2:3, :] = gain_sum + jnp.sum(total * unit_in, axis=0, keepdims=True)
+            delta_inner = norm_back(total, unit_in, scale_in, gain_ref[...])
+            delta_inner_ref[...] = delta_inner
+            delta_iso_ref[...] = keep_rows(delta_inner * (1.0 - act_in * act_in), n).astype(BF)
+
+        both(meta_ref, lambda: run(0), lambda: run(1))
+
+    return call(
+        kernel,
+        [SMEM] + vmem(6) + [ANY] + vmem(2),
+        [
+            ((length, features), F32),
+            ((shards, rows, features), BF),
+            ((rows, features), BF),
+            ((rows, features), F32),
+            ((8, features), F32),
+        ],
+        [
+            pltpu.VMEM((shards * plan.down_max, features), BF),
+            split(plan.stage_rows, features),
+            pltpu.VMEM((length, features), F32),
+            pltpu.SemaphoreType.DMA((shards,)),
+        ],
+        flops=2 * rows * features * features * SCALE_L,
+        moved=16 << 20,
+        limit=52,
+    )(meta, up_keep, up_recv, series, act, act_iso, low, trans, biases, gain)
+
+
+def trans_weight(plan, meta, inner_all, own_taps, other_taps):
+    shards, rows, features = plan.shards, plan.rows, plan.features
+
+    def kernel(meta_ref, inner_ref, own_ref, other_ref, grad_ref, total):
+        lhs = inner_ref[...]
+
+        def run(b):
+            own = plan.down_rows[b]
+            odd = meta_ref[5]
+            first = dot(lhs, own_ref[...], ((0,), (0,)))
+            total[pl.ds(pl.multiple_of(odd * features, 8), features), :] = first
+            if own != features:
+                second = dot(lhs, other_ref[...], ((0,), (0,)))
+                total[pl.ds(pl.multiple_of((1 - odd) * features, 8), features), :] = second
+            start = pl.multiple_of(meta_ref[6], 8)
+            grad_ref[0:own, :] = total[pl.ds(start, own), :].astype(BF)
+
+        both(meta_ref, lambda: run(0), lambda: run(1))
+
+    flat = (shards * rows, features)
+    return call(
+        kernel,
+        [SMEM] + vmem(3),
+        [((plan.down_max, features), BF)],
+        [pltpu.VMEM((2 * features, features), F32)],
+        flops=4 * shards * rows * features * features,
+        moved=5 << 20,
+        limit=32,
+    )(meta, inner_all.reshape(flat), own_taps.reshape(flat), other_taps.reshape(flat))[0]
+
+
+def down_delta(plan, meta, pieces, delta_inner, act):
+    rows, features = plan.rows, plan.features
+    count = len(pieces)
+
+    def kernel(meta_ref, *refs):
+        parts = refs[:count]
+        inner_ref, act_ref, out_ref = refs[count:]
+        total = parts[0][...] + inner_ref[...]
+        for piece in parts[1:]:
+            total = total + piece[...].astype(F32)
+        value = act_ref[...]
+        out_ref[...] = keep_rows(total * (1.0 - value * value), meta_ref[4]).astype(BF)
+
+    return call(
+        kernel,
+        [SMEM] + vmem(count + 2),
+        [((rows, features), BF)],
+        [],
+        moved=1 << 19,
+        limit=16,
+    )(meta, *pieces, delta_inner, act)[0]
+
+
+def input_delta(plan, meta, delta_down, outer, down):
+    features, length = plan.features, plan.length
+
+    def kernel(meta_ref, delta_ref, outer_ref, w_hbm, out_ref, weight, stage, sems):
+        def run(b):
+            k, n = plan.factors[b], plan.steps[b]
+            copies = fetch_weight(plan, b, w_hbm, weight, sems)
+            for copy in copies:
+                copy.wait()
+            fit = up8(n)
+            value = delta_ref[...]
+            for j in range(k):
+                part = dot(value, weight[j * features : (j + 1) * features, :], ((1,), (1,)))
+                put(stage, j, part[:fit], k)
+            margin = k // 2
+            out_ref[...] = (get(stage, margin, length) + outer_ref[...]).astype(BF)
+
+        both(meta_ref, lambda: run(0), lambda: run(1))
+
+    return call(
+        kernel,
+        [SMEM] + vmem(2) + [ANY],
+        [((length, features), BF)],
+        [
+            pltpu.VMEM((plan.shards * plan.down_max, features), BF),
+            split(plan.stage_rows, features),
+            pltpu.SemaphoreType.DMA((plan.shards,)),
+        ],
+        flops=2 * plan.rows * features * features * SCALE_L,
+        moved=12 << 20,
+        limit=40,
+    )(meta, delta_down, outer, down)[0]
+
+
+def down_weight(plan, meta, matrix, delta_slots):
+    shards, rows, features = plan.shards, plan.rows, plan.features
+    count = len(delta_slots)
+
+    def kernel(meta_ref, a_ref, *refs):
+        delta_refs = slot_list(refs[:count], plan)
+        grad_ref, sum_ref, delta, ordered = refs[count:]
+        me = meta_ref[1]
+        for q in range(shards):
+            value = delta_refs[q][...].astype(F32)
+            ordered[pl.ds(me ^ plan.mask(q), 1), :] = jnp.sum(value, axis=0, keepdims=True)
+            delta[q * rows : (q + 1) * rows, :] = value
+        sum_ref[...] = jnp.sum(ordered[...], axis=0, keepdims=True)
+        grad_ref[...] = dot(a_ref[...], delta[...].astype(BF), ((0,), (0,))).astype(BF)
+
+    return call(
+        kernel,
+        [SMEM] + vmem(1 + count),
+        [((plan.down_max, features), BF), ((1, features), F32)],
+        [pltpu.VMEM((shards * rows, features), F32), pltpu.VMEM((shards, features), F32)],
+        flops=2 * shards * rows * features * features,
+        moved=4 << 20,
+        limit=32,
+    )(meta, matrix, *delta_slots)
+
+
+def hop(values, distance, shards):
+    return lax.ppermute(values, "series", [(i, i ^ distance) for i in range(shards)])
+
+
+def swap(values):
+    return lax.ppermute(values, "branch", [(0, 1), (1, 0)])
+
+
+def gather_slots(plan, own):
+    shards = plan.shards
+    line = [own] + [hop(own, i << 2, shards) for i in range(1, plan.quarter)]
+    side = [hop(value, 2, shards) for value in line]
+    return line + side + [hop(jnp.stack(line + side), 1, shards)]
+
+
+def scatter_sum(plan, keep, send):
+    shards, quarter = plan.shards, plan.quarter
+    first = keep + hop(send, 1, shards).astype(F32)
+    second = first[:quarter] + hop(first[quarter:].astype(BF), 2, shards).astype(F32)
+    pieces = [second[0]]
+    for i in range(1, quarter):
+        pieces.append(hop(second[i].astype(BF), i << 2, shards))
+    return pieces
+
+
+def rounded(values):
+    return lax.reduce_precision(values, exponent_bits=8, mantissa_bits=7)
 
 
 def layer_norm(values, gain_row, shift_row):
@@ -21,19 +643,194 @@
     return jax.nn.gelu(values, approximate=False)
 
 
-def product(first_operand, second_operand):
-    return jnp.dot(first_operand, second_operand, preferred_element_type=jnp.float32)
-
-
-def left_product(first_operand, second_operand):
-    return jnp.einsum(
-        "mi,mo->io", first_operand, second_operand, preferred_element_type=jnp.float32
-    )
-
-
-def right_product(first_operand, second_operand):
-    return jnp.einsum(
-        "mo,io->mi", first_operand, second_operand, preferred_element_type=jnp.float32
+def product(a, b):
+    return jnp.dot(a, b, preferred_element_type=F32)
+
+
+def left_product(a, b):
+    return jnp.einsum("mi,mo->io", a, b, preferred_element_type=F32)
+
+
+def right_product(a, b):
+    return jnp.einsum("mo,io->mi", a, b, preferred_element_type=F32)
+
+
+def body(
+    series_in, target, horizons, observed,
+    down_short, iso_short, trans_short, down_long, iso_long, trans_long,
+    branch_bias, branch_gain, merge_weight, head_bias, head_gain, ff_in, ff_in_bias, ff_out,
+):
+    shards = lax.axis_size("series")
+    _, length, features = series_in.shape
+    plan = Plan(
+        shards,
+        length,
+        features,
+        (down_short.shape[0], down_long.shape[0]),
+        (iso_short.shape[0], iso_long.shape[0]),
+    )
+    half_rows = length // 2
+    branch = lax.axis_index("branch")
+    me = lax.axis_index("series")
+    is_short = branch == 0
+    iso_rows = jnp.where(is_short, plan.iso_rows[0], plan.iso_rows[1])
+    down_rows = jnp.where(is_short, plan.down_rows[0], plan.down_rows[1])
+    meta = jnp.stack(
+        [
+            branch,
+            me,
+            (me * iso_rows) // features,
+            (me * iso_rows) % features,
+            jnp.where(is_short, plan.steps[0], plan.steps[1]),
+            me % 2,
+            (2 * down_rows * (me // 2)) % features + (me % 2) * down_rows,
+            0,
+        ]
+    ).astype(jnp.int32)
+    series = series_in[0]
+    biases, gain = branch_bias[0], branch_gain
+
+    def chosen(short, long):
+        rows = max(short.shape[0], long.shape[0])
+        short = jnp.pad(short, ((0, rows - short.shape[0]), (0, 0)))
+        long = jnp.pad(long, ((0, rows - long.shape[0]), (0, 0)))
+        return jnp.where(is_short, short, long)
+
+    own_trans = chosen(trans_short, trans_long)
+    trans_all = lax.all_gather(own_trans, "series", axis=0)
+
+    blocks = lax.all_to_all(
+        prep_blocks(plan, meta, series), "series", split_axis=0, concat_axis=0, tiled=True
+    )
+    keep, send, matrix = down_partial(plan, meta, blocks, down_short, down_long)
+    low, act_down = low_rows(plan, meta, scatter_sum(plan, keep, send), biases)
+    low_slots = gather_slots(plan, low)
+    keep, send = iso_partial(plan, meta, low_slots, iso_short, iso_long, False)
+    pieces = scatter_sum(plan, keep, send)
+    out_keep, out_send, act_trans, inner, act_iso = branch_forward(
+        plan, meta, pieces, low, series, trans_all, biases, gain
+    )
+    out_recv = swap(out_send)
+    own_down, _ = lax.optimization_barrier((chosen(down_short, down_long), out_keep))
+    down_all = lax.all_gather(own_down, "series", axis=0)
+
+    merge_own = lax.dynamic_index_in_dim(merge_weight, branch, 0, keepdims=False)
+    merge_other = lax.dynamic_index_in_dim(merge_weight, 1 - branch, 0, keepdims=False)
+    merged = product(out_keep, merge_own) + product(out_recv, merge_other) + head_bias[0]
+    normed, first_back = jax.vjp(layer_norm, merged, head_gain[0], head_bias[2])
+    low_normed = normed.astype(BF)
+    pre_ff = product(low_normed, ff_in) + ff_in_bias
+    activated, gelu_back = jax.vjp(gelu_exact, pre_ff)
+    low_act = activated.astype(BF)
+    ff_result = product(low_act, ff_out) + head_bias[1]
+    final_out, second_back = jax.vjp(layer_norm, merged + ff_result, head_gain[1], head_bias[3])
+    positions = branch * half_rows + jnp.arange(half_rows, dtype=jnp.int32)
+    observed_half = lax.dynamic_slice_in_dim(observed[0], branch * half_rows, half_rows, 0)
+    valid = (
+        observed_half.astype(F32)
+        * (positions >= SEQ_IN).astype(F32)
+        * (positions < SEQ_IN + horizons[0]).astype(F32)
+    )
+    error_rows = final_out - target[0].astype(F32)
+    weighted = valid[:, None] * error_rows
+    loss_part = 0.5 * jnp.sum(weighted * error_rows) / (features * length)
+    delta_sum, gain_second, shift_second = second_back(weighted)
+    delta_ff = delta_sum.astype(BF)
+    grad_ff_out = left_product(low_act, delta_ff)
+    delta_act = right_product(delta_ff, ff_out)
+    (delta_pre,) = gelu_back(delta_act)
+    low_pre = delta_pre.astype(BF)
+    grad_ff_in = left_product(low_pre, low_normed)
+    delta_normed = right_product(low_pre, ff_in)
+    delta_first, gain_first, shift_first = first_back(delta_normed)
+    delta_merged = (delta_first + delta_sum).astype(BF)
+    grad_merge_own = left_product(out_keep, delta_merged)
+    grad_merge_other = left_product(out_recv, delta_merged)
+    up_keep = right_product(delta_merged, merge_own).astype(BF)
+    up_send = right_product(delta_merged, merge_other).astype(BF)
+    up_recv = swap(up_send)
+
+    outer, taps, delta_iso, delta_inner, vectors = branch_backward(
+        plan, meta, up_keep, up_recv, series, act_trans, act_iso, low, trans_all, biases, gain
+    )
+    delta_slots = gather_slots(plan, delta_iso)
+    keep, send = iso_partial(plan, meta, delta_slots, iso_short, iso_long, True)
+    pieces = scatter_sum(plan, keep, send)
+    grad_iso, iso_sum = iso_weight(plan, meta, low_slots, delta_slots)
+    iso_recv = swap(grad_iso)
+    delta_down = down_delta(plan, meta, pieces, delta_inner, act_down)
+    down_slots = gather_slots(plan, delta_down)
+    input_own = input_delta(plan, meta, delta_down, outer, down_all)
+    input_recv = swap(input_own)
+    grad_down, down_sum = down_weight(plan, meta, matrix, down_slots)
+    down_recv = swap(grad_down)
+
+    inner_all = lax.all_gather(inner, "series", axis=0)
+    own_taps = lax.all_to_all(taps, "series", split_axis=0, concat_axis=0, tiled=True)
+    grad_trans = trans_weight(plan, meta, inner_all, own_taps, hop(own_taps, 1, shards))
+    trans_recv = swap(grad_trans)
+
+    def placed(own, other, b, rows):
+        return jnp.where(branch == b, own, other)[:rows].astype(F32)
+
+    ff_in_share = rounded(
+        lax.psum_scatter(grad_ff_in, "series", scatter_dimension=0, tiled=True)
+    )
+    ff_out_share = rounded(
+        lax.psum_scatter(grad_ff_out, "series", scatter_dimension=0, tiled=True)
+    )
+    ff_in_total = ff_in_share + swap(ff_in_share.astype(BF)).astype(F32)
+    ff_out_total = ff_out_share + swap(ff_out_share.astype(BF)).astype(F32)
+    loss = loss_part[None] + swap(loss_part[None])
+    short_own = jnp.where(is_short, 1.0, 0.0)
+    head_rows = jnp.stack(
+        [
+            jnp.sum(delta_merged.astype(F32), axis=0),
+            jnp.sum(delta_ff.astype(F32), axis=0),
+            shift_first,
+            shift_second,
+            gain_first,
+            gain_second,
+        ]
+    )
+    ff_bias_grad = jnp.sum(low_pre.astype(F32), axis=0)
+    selector = jnp.stack([short_own, 1.0 - short_own])
+    branch_rows = (selector[:, None, None] * vectors[None, 0:3]).reshape(6, features)
+    merge_pair = jnp.where(
+        is_short,
+        jnp.stack([grad_merge_own, grad_merge_other]),
+        jnp.stack([grad_merge_other, grad_merge_own]),
+    )
+    merge_total = lax.psum(merge_pair, ("branch", "series"))
+    small = jnp.concatenate([head_rows, ff_bias_grad.reshape(-1, features), branch_rows], axis=0)
+    small = lax.psum(small, ("branch", "series"))
+    ff_rows = ff_in_bias.shape[0] // features
+    branch_total = small[6 + ff_rows :].reshape(2, 3, features)
+    late = jnp.concatenate([down_sum, iso_sum], axis=0)
+    late_recv = swap(late)
+    late_short = jnp.where(is_short, late, late_recv)
+    late_long = jnp.where(is_short, late_recv, late)
+    late_all = jnp.stack([late_short, late_long])
+    bias_total = jnp.concatenate([late_all, branch_total[:, 0:2]], axis=1)
+
+    return (
+        final_out.astype(BF)[None],
+        loss,
+        (input_own.astype(F32) + input_recv.astype(F32))[None],
+        placed(grad_down, down_recv, 0, plan.down_rows[0]),
+        placed(grad_iso, iso_recv, 0, plan.iso_rows[0]),
+        placed(grad_trans, trans_recv, 0, plan.down_rows[0]),
+        placed(grad_down, down_recv, 1, plan.down_rows[1]),
+        placed(grad_iso, iso_recv, 1, plan.iso_rows[1]),
+        placed(grad_trans, trans_recv, 1, plan.down_rows[1]),
+        bias_total,
+        branch_total[:, 2],
+        merge_total,
+        small[0:4],
+        small[4:6],
+        ff_in_total.T,
+        small[6 : 6 + ff_rows].reshape(-1),
+        ff_out_total,
     )
 
 
@@ -175,7 +972,7 @@
     return (delta_series, padded_grads, vectors, gain_inner + gain_outer)
 
 
-def body(
+def plain_body(
     series_in,
     target,
     horizons,
@@ -374,28 +1171,42 @@
         P(),
         P(),
     )
-    return jax.shard_map(
-        body,
-        mesh=mesh,
-        in_specs=placed,
-        out_specs=(
-            P("series", "branch", None),
-            P("series"),
-            P("series", None, None),
-            P("series", None),
-            P("series", None),
-            P("series", None),
-            P("series", None),
-            P("series", None),
-            P("series", None),
-            P(),
-            P(),
-            P(),
-            P(),
-            P(),
-            P(None, "series"),
-            P(),
-            P("series", None),
-        ),
-        check_vma=False,
-    )
+
+    def run(*args):
+        shards = mesh.shape["series"]
+        features = args[0].shape[2]
+        fits = (
+            args[0].shape[0] == shards
+            and shards >= 8
+            and shards & (shards - 1) == 0
+            and all((args[i].shape[0] // shards) % LANE == 0 for i in (4, 7))
+            and all((args[i].shape[0] // shards) % 16 == 0 for i in (5, 8))
+            and all(2 * (args[i].shape[0] // shards) + features // 2 <= 3 * features for i in (4, 7))
+        )
+        return jax.shard_map(
+            body if fits else plain_body,
+            mesh=mesh,
+            in_specs=placed,
+            out_specs=(
+                P("series", "branch", None),
+                P("series"),
+                P("series", None, None),
+                P("series", None),
+                P("series", None),
+                P("series", None),
+                P("series", None),
+                P("series", None),
+                P("series", None),
+                P(),
+                P(),
+                P(),
+                P(),
+                P(),
+                P(None, "series"),
+                P(),
+                P("series", None),
+            ),
+            check_vma=False,
+        )(*args)
+
+    return run

time: 2380 us -> 607 us (0.26)
  waiting for transfers between devices: 1610 us -> 266 us
  local copies, waits for them, and re-layouts: 342 us -> 39.7 us
  other arithmetic: 176 us -> 37.7 us
  matrix products: 145 us -> 31 us
  starting transfers between devices: 4.73 us -> 68.3 us
  Pallas kernels: 0 us -> 53.6 us
    reduce_scatter x4 -> x1, waiting for transfers between devices: 1030 us -> 0.02 us  [body(): lax.psum_scatter(grad_ff_in, 'series', scatter_dimension=0, tiled=True)]
    all_gather x3, waiting for transfers between devices: 329 us -> 0.01 us  [the longest x1 0.01 us: body(): trans_all = lax.all_gather(own_trans, 'series', axis=0)]
    ppermute x0 -> x50, waiting for transfers between devices: none -> 124 us  [the longest x40 94.2 us: hop(): lax.ppermute(values, 'series', [(i, i ^ distance) for i in range(shards)])]
    dot_general x21 -> x12, matrix products: 145 us -> 31 us  [the longest x4 12 us: product(): return jnp.dot(a, b, preferred_element_type=F32)]
    psum x2 -> x1, waiting for transfers between devices: 239 us -> 128 us  [body(): merge_total = lax.psum(merge_pair, ('branch', 'series'))]
    scatter-add x68 -> x0, local copies, waits for them, and re-layouts: 106 us -> none  [branch_back(): delta_padded.at[:, offset:offset + step_count]]
    add x70 -> x4, other arithmetic: 105 us -> 3.76 us  [the longest x3 2.07 us: scatter_sum(): first = keep + hop(send, 1, shards).astype(F32)]
    ppermute x0 -> x50, starting transfers between devices: none -> 63.5 us  [the longest x40 50.9 us: hop(): lax.ppermute(values, 'series', [(i, i ^ distance) for i in range(shards)])]
  transfers between devices with their start and end apart: 11 -> 57, of which waited for: 9 -> 29; matrix products, arithmetic and copies ran while one was open for 22% -> 13% of each run, Pallas kernels for 0% -> 8%
where the time goes in v1:
time: 607 us; the launch traced here: 598 us
  waiting for transfers between devices  266 us (44%)
  blocking collectives  82.2 us (14%)
  starting transfers between devices  68.3 us (11%)
  Pallas kernels  53.6 us (9%)
  local copies, waits for them, and re-layouts  39.7 us (7%)
  other arithmetic  37.7 us (6%)
  matrix products  31 us (5%)
  between operations  18.9 us (3%)
    psum x1, waiting for transfers between devices, body(): merge_total = lax.psum(merge_pair, ('branch', 'series'))  128 us
    ppermute x40, waiting for transfers between devices, hop(): lax.ppermute(values, 'series', [(i, i ^ distance) for i in range(shards)])  94.2 us
    ppermute x40, starting transfers between devices, hop(): lax.ppermute(values, 'series', [(i, i ^ distance) for i in range(shards)])  50.9 us
    all_to_all x1, blocking collectives, body(): lax.all_to_all(prep_blocks(plan, meta, series), 'series', split_axis=0, c...  43.3 us
    psum x1, blocking collectives, body(): small = lax.psum(small, ('branch', 'series'))  38.9 us
    unnamed x204, local copies, waits for them, and re-layouts  35.9 us
    ppermute x10, waiting for transfers between devices, swap(): return lax.ppermute(values, 'branch', [(0, 1), (1, 0)])  30 us
    pallas_call x2, Pallas kernels, iso_partial(): call(kernel, [SMEM] + vmem(count + 2), [((half, rows, features), F32), ((...  15.1 us
  transfers between devices with their start and end apart: 57, of which 29 were waited for; matrix products, arithmetic and copies ran while one was open for 13% of the time, Pallas kernels for 8%

profile of v1, /device:TPU:0, one launch (start us, length us, event | category | flops | bytes accessed | tf_op | source)
XLA Modules:
  0.0 597.7 jit_solution(7327412022838406391)
XLA Ops:
  11.7 43.3 %all_to_all.10.in_ref = bf16[16,208,128]{2,1,0:T(8,128)(2,1)S(1)} all-to-all(bf16[16,208,128]{2,1,0:T(8,128)(2,1)S(1)} %shard_map.305), channel_id=1, replica_groups=mesh['branch'=2,'series'=16] {'series'}, dimensions={0} | all-to-all | bytes 1703936 | tf_op jit(solution)/shard_map/all_to_all | solution.py:702
  62.2 13.1 %collective-permute-done.1 = bf16[4,72,512]{2,1,0:T(8,128)(2,1)S(1)} collective-permute-done((bf16[4,72,512]{2,1,0:T(8,128)(2,1)S(1)}, bf16[4,72,512]{2,1,0:T(8,128)(2,1)S(1)}, u32[]{:S(2)}, u32[]{:S(2)}) %collective-permute-start.1) | collective-permute-done | bytes 294944 | tf_op jit(solution)/shard_map/ppermute | solution.py:608
  79.9 5.2 collective-permute-done.2.refs_1_
  85.0 5.3 collective-permute-done.3.refs_2_
  91.0 4.9 collective-permute-start.5
  104.5 4.2 collective-permute-done.6.refs_2_
  116.9 7.1 %shard_map.308 = (f32[8,72,512]{2,1,0:T(8,128)S(1)}, bf16[8,72,512]{2,1,0:T(8,128)(2,1)S(1)}) custom-call(s32[8]{0:T(128)S(1)} %stack.154.meta_ref, bf16[72,512]{1,0:T(8,128)(2,1)S(1)} %get-tuple-element.43.refs_0_.refs_4_.low_ref, bf16[72,512]{1,0:T(8,128)(2,1)S(1)} %collective-permute-done.5.refs_1_, bf16[72,512]{1,0:T(8,128)(2,1)S(1)} %collective-permute-done.6.refs_2_, ...), custom_call_target="tpu_custom_call" | custom-call | flops 3623878656 | bytes 10485760 | tf_op jit(solution)/shard_map/pallas_call | solution.py:278
  128.0 8.3 %collective-permute-done.14 = bf16[4,72,512]{2,1,0:T(8,128)(2,1)S(1)} collective-permute-done((bf16[4,72,512]{2,1,0:T(8,128)(2,1)S(1)}, bf16[4,72,512]{2,1,0:T(8,128)(2,1)S(1)}, u32[]{:S(2)}, u32[]{:S(2)}) %collective-permute-start.14) | collective-permute-done | bytes 294944 | tf_op jit(solution)/shard_map/ppermute | solution.py:608
  142.4 4.7 collective-permute-done.16.refs_2_
  151.1 5.3 shard_map.309
  165.1 8.4 %collective-permute-done.18 = bf16[408,512]{1,0:T(8,128)(2,1)S(1)} collective-permute-done((bf16[408,512]{1,0:T(8,128)(2,1)}, bf16[408,512]{1,0:T(8,128)(2,1)S(1)}, u32[]{:S(2)}, u32[]{:S(2)}) %collective-permute-start.18) | collective-permute-done | bytes 417824 | tf_op jit(solution)/shard_map/ppermute | solution.py:612
  176.9 7.7 %multiply_convert_fusion = (bf16[408,2048]{1,0:T(8,128)(2,1)S(1)}, f32[408,2048]{1,0:T(8,128)S(1)}, f32[408,2048]{1,0:T(8,128)S(1)}) fusion(f32[2048]{0:T(1024)S(1)} %copy-done.87, bf16[512,2048]{1,0:T(8,128)(2,1)S(1)} %copy-done, f32[408,512]{1,0:T(8,128)S(1)} %get-tuple-element.145, f32[512]{0:T(512)S(1)} %bitcast.193, f32[512]{0:T(512)S(1)} %bitcast.185, ...), kind=kOutput, calls=%fused_computation.4 | convolution fusion | flops 911831040 | bytes 11304128 | tf_op jit(solution)/shard_map/dot_general | solution.py:647
  214.5 9.2 %shard_map.310 = (f32[816,512]{1,0:T(8,128)}, bf16[16,72,512]{2,1,0:T(8,128)(2,1)}, bf16[72,512]{1,0:T(8,128)(2,1)S(1)}, f32[72,512]{1,0:T(8,128)S(1)}, f32[8,512]{1,0:T(8,128)S(1)}) custom-call(s32[8]{0:T(128)S(1)} %stack.154.meta_ref, bf16[408,512]{1,0:T(8,128)(2,1)S(1)} %convolution_convert_fusion.1.uk_ref, ...), custom_call_target="tpu_custom_call" | custom-call | flops 603979776 | bytes 16777216 | tf_op jit(solution)/shard_map/pallas_call | solution.py:471
  243.8 8.0 %shard_map.311 = (f32[8,72,512]{2,1,0:T(8,128)S(1)}, bf16[8,72,512]{2,1,0:T(8,128)(2,1)}) custom-call(s32[8]{0:T(128)S(1)} %stack.154.meta_ref, bf16[72,512]{1,0:T(8,128)(2,1)S(1)} %get-tuple-element.50.refs_0_.refs_9_, bf16[72,512]{1,0:T(8,128)(2,1)S(1)} %collective-permute-done.21.refs_1_.refs_10_, ...), custom_call_target="tpu_custom_call" | custom-call | flops 3623878656 | bytes 10485760 | tf_op jit(solution)/shard_map/pallas_call | solution.py:278
  253.8 4.4 all-to-all-start.1
  262.1 9.7 %shard_map.315 = (bf16[2208,512]{1,0:T(8,128)(2,1)}, f32[1,512]{1,0:T(1,128)S(1)}) custom-call(s32[8]{0:T(128)S(1)} %stack.154.meta_ref, bf16[72,512]{1,0:T(8,128)(2,1)S(1)} %get-tuple-element.43.refs_0_.refs_4_.low_ref, bf16[72,512]{1,0:T(8,128)(2,1)S(1)} %copy-done.29, bf16[72,512]{1,0:T(8,128)(2,1)S(1)} %copy-done.31, bf16[72,512]{1,0:T(8,128)(2,1)S(1)} %copy-done.33, ...), custom_call_target="tpu_custom_call" | custom-call | flops 3623878656 | bytes 10485760 | tf_op jit(solution)/shard_map/pallas_call | solution.py:325
  279.1 12.0 %collective-permute-done.31.refs_1_ = bf16[72,512]{1,0:T(8,128)(2,1)S(1)} collective-permute-done((bf16[72,512]{1,0:T(8,128)(2,1)S(1)}, bf16[72,512]{1,0:T(8,128)(2,1)S(1)}, u32[]{:S(2)}, u32[]{:S(2)}) %collective-permute-start.31) | collective-permute-done | bytes 73760 | tf_op jit(solution)/shard_map/ppermute | solution.py:608
  291.1 12.8 %collective-permute-done.32.refs_2_ = bf16[72,512]{1,0:T(8,128)(2,1)S(1)} collective-permute-done((bf16[72,512]{1,0:T(8,128)(2,1)S(1)}, bf16[72,512]{1,0:T(8,128)(2,1)S(1)}, u32[]{:S(2)}, u32[]{:S(2)}) %collective-permute-start.32) | collective-permute-done | bytes 73760 | tf_op jit(solution)/shard_map/ppermute | solution.py:608
  332.8 38.9 %psum.14 = f32[16,512]{1,0:T(8,128)S(1)} all-reduce(f32[16,512]{1,0:T(8,128)S(1)} %concatenate.10), channel_id=1, replica_groups=mesh['branch'=2,'series'=16] {'branch','series'}, use_global_device_ids=true, to_apply=%region_16.17 | all-reduce | flops 8192 | bytes 65536 | tf_op jit(solution)/shard_map/psum | solution.py:806
  382.9 8.7 %collective-permute-done.47 = f32[2,512]{1,0:T(2,128)S(1)} collective-permute-done((f32[2,512]{1,0:T(2,128)S(1)}, f32[2,512]{1,0:T(2,128)S(1)}, u32[]{:S(2)}, u32[]{:S(2)}) %collective-permute-start.47) | collective-permute-done | bytes 4128 | tf_op jit(solution)/shard_map/ppermute | solution.py:612
  408.9 8.3 %collective-permute-done.46 = bf16[512,512]{1,0:T(8,128)(2,1)S(1)} collective-permute-done((bf16[512,512]{1,0:T(8,128)(2,1)S(1)}, bf16[512,512]{1,0:T(8,128)(2,1)S(1)}, u32[]{:S(2)}, u32[]{:S(2)}) %collective-permute-start.46) | collective-permute-done | bytes 524320 | tf_op jit(solution)/shard_map/ppermute | solution.py:612
  424.2 5.9 shard_map.313
  433.3 14.2 %reduce-scatter.5.cloned.1.call-done = f32[128,512]{1,0:T(8,128)} async-done(((f32[2048,512]{1,0:T(8,128)}), f32[128,512]{1,0:T(8,128)}) %reduce-scatter.5.cloned.1.call-update) | async-done | bytes 262160 | tf_op jit(solution)/shard_map/reduce_scatter | solution.py:780
  458.6 127.6 %all-reduce.4.cloned.1.call-done = f32[2,512,512]{2,1,0:T(8,128)} async-done(((f32[2,512,512]{2,1,0:T(8,128)}), f32[2,512,512]{2,1,0:T(8,128)}) %all-reduce.4.cloned.1.call-update) | async-done | bytes 2097168 | tf_op jit(solution)/shard_map/psum | solution.py:804
  (395 shorter events, 201.6 us)
Async XLA Ops:
  7.2 141.1 %all-gather.7.cloned.1.call-start = ((), (), s32[]{:S(2)}) async-start(), calls=%async_computation.7 | async-start | bytes 8912896 | tf_op jit(solution)/shard_map/all_gather | solution.py:700
  9.4 390.9 %all-gather.11.cloned.1.call-start = ((), (), s32[]{:S(2)}) async-start(), calls=%async_computation.9 | async-start | bytes 1253376 | tf_op jit(solution)/shard_map/all_gather | solution.py:768
  60.3 15.0 %collective-permute-start.1 = (bf16[4,72,512]{2,1,0:T(8,128)(2,1)S(1)}, bf16[4,72,512]{2,1,0:T(8,128)(2,1)S(1)}, u32[]{:S(2)}, u32[]{:S(2)}) collective-permute-start(bf16[4,72,512]{2,1,0:T(8,128)(2,1)S(1)} %slice.211), channel_id=1, source_target_pairs={{0,2},{1,3},{2,0},{3,1},{4,6},{5,7},{6,4},{7,5},{8,10},{9,11},{10,... | collective-permute-start | bytes 884744 | tf_op jit(solution)/shard_map/ppermute | solution.py:608
  77.3 13.1 %collective-permute-start.3 = (bf16[72,512]{1,0:T(8,128)(2,1)S(1)}, bf16[72,512]{1,0:T(8,128)(2,1)S(1)}, u32[]{:S(2)}, u32[]{:S(2)}) collective-permute-start(bf16[72,512]{1,0:T(8,128)(2,1)S(1)} %get-tuple-element.132), channel_id=1, source_target_pairs={{0,8},{1,9},{2,10},{3,11},{4,12},{5,13},{6,14},{7,15},{8,0},{9,1},... | collective-permute-start | bytes 221192 | tf_op jit(solution)/shard_map/ppermute | solution.py:608
  78.3 12.0 %collective-permute-start.4 = (bf16[72,512]{1,0:T(8,128)(2,1)S(1)}, bf16[72,512]{1,0:T(8,128)(2,1)S(1)}, u32[]{:S(2)}, u32[]{:S(2)}) collective-permute-start(bf16[72,512]{1,0:T(8,128)(2,1)S(1)} %get-tuple-element.131), channel_id=1, source_target_pairs={{0,12},{1,13},{2,14},{3,15},{4,8},{5,9},{6,10},{7,11},{8,4},{9,5},... | collective-permute-start | bytes 221192 | tf_op jit(solution)/shard_map/ppermute | solution.py:608
  95.9 12.8 %collective-permute-start.6 = (bf16[72,512]{1,0:T(8,128)(2,1)S(1)}, bf16[72,512]{1,0:T(8,128)(2,1)S(1)}, u32[]{:S(2)}, u32[]{:S(2)}) collective-permute-start(bf16[72,512]{1,0:T(8,128)(2,1)S(1)} %get-tuple-element.43.refs_0_.refs_4_.low_ref), channel_id=1, source_target_pairs={{0,8},{1,9},{2,10},{3,11},{4,12},{5,13},{6,14},{7,15},{8,0},{9,1},... | collective-permute-start | bytes 221192 | tf_op jit(solution)/shard_map/ppermute | solution.py:608
  95.9 14.6 %collective-permute-start.7 = (bf16[72,512]{1,0:T(8,128)(2,1)S(1)}, bf16[72,512]{1,0:T(8,128)(2,1)S(1)}, u32[]{:S(2)}, u32[]{:S(2)}) collective-permute-start(bf16[72,512]{1,0:T(8,128)(2,1)S(1)} %get-tuple-element.43.refs_0_.refs_4_.low_ref), channel_id=1, source_target_pairs={{0,12},{1,13},{2,14},{3,15},{4,8},{5,9},{6,10},{7,11},{8,4},{9,5},... | collective-permute-start | bytes 221192 | tf_op jit(solution)/shard_map/ppermute | solution.py:608
  98.3 12.5 %collective-permute-start.8 = (bf16[72,512]{1,0:T(8,128)(2,1)S(1)}, bf16[72,512]{1,0:T(8,128)(2,1)S(1)}, u32[]{:S(2)}, u32[]{:S(2)}) collective-permute-start(bf16[72,512]{1,0:T(8,128)(2,1)S(1)} %get-tuple-element.43.refs_0_.refs_4_.low_ref), channel_id=1, source_target_pairs={{0,2},{1,3},{2,0},{3,1},{4,6},{5,7},{6,4},{7,5},{8,10},{9,11},{10,... | collective-permute-start | bytes 221192 | tf_op jit(solution)/shard_map/ppermute | solution.py:608
  159.6 259.6 %all-gather.9.cloned.1.call-start = ((), (), s32[]{:S(2)}) async-start(), calls=%async_computation.8 | async-start | bytes 8912896 | tf_op jit(solution)/shard_map/all_gather | solution.py:715
  161.7 268.6 %reduce-scatter.3.cloned.1.call-start = ((), (), s32[]{:S(2)}) async-start(), calls=%async_computation.5 | async-start | bytes 4456448 | tf_op jit(solution)/shard_map/reduce_scatter | solution.py:777
  198.2 249.3 %reduce-scatter.5.cloned.1.call-start = ((), (), s32[]{:S(2)}) async-start(), calls=%async_computation.6 | async-start | bytes 4456448 | tf_op jit(solution)/shard_map/reduce_scatter | solution.py:780
  253.8 129.1 %all-to-all-start.1 = ((bf16[16,72,512]{2,1,0:T(8,128)(2,1)}), bf16[16,72,512]{2,1,0:T(8,128)(2,1)}, u32[]{:S(2)}, u32[]{:S(2)}) async-start(bf16[16,72,512]{2,1,0:T(8,128)(2,1)} %get-tuple-element.61), calls=%async_computation.1 | async-start | bytes 2359296 | tf_op jit(solution)/shard_map/all_to_all | solution.py:769
  258.2 328.0 %all-reduce.4.cloned.1.call-start = ((), (), s32[]{:S(2)}) async-start(), calls=%async_computation.4 | async-start | bytes 4194304 | tf_op jit(solution)/shard_map/psum | solution.py:804
  260.1 14.4 %collective-permute-start.30 = (bf16[4,72,512]{2,1,0:T(8,128)(2,1)S(1)}, bf16[4,72,512]{2,1,0:T(8,128)(2,1)S(1)}, u32[]{:S(2)}, u32[]{:S(2)}) collective-permute-start(bf16[4,72,512]{2,1,0:T(8,128)(2,1)S(1)} %slice.209), channel_id=1, source_target_pairs={{0,2},{1,3},{2,0},{3,1},{4,6},{5,7},{6,4},{7,5},{8,10},{9,11},{10,... | collective-permute-start | bytes 884744 | tf_op jit(solution)/shard_map/ppermute | solution.py:608
  271.7 124.5 %collective-permute-start.44 = (bf16[2208,512]{1,0:T(8,128)(2,1)}, bf16[2208,512]{1,0:T(8,128)(2,1)}, u32[]{:S(2)}, u32[]{:S(2)}) collective-permute-start(bf16[2208,512]{1,0:T(8,128)(2,1)} %get-tuple-element.59), channel_id=1, source_target_pairs={{0,16},{16,0},{1,17},{17,1},{2,18},{18,2},{3,19},{19,3},{4,20},{20... | collective-permute-start | bytes 6782984 | tf_op jit(solution)/shard_map/ppermute | solution.py:612
  274.6 16.5 %collective-permute-start.31 = (bf16[72,512]{1,0:T(8,128)(2,1)S(1)}, bf16[72,512]{1,0:T(8,128)(2,1)S(1)}, u32[]{:S(2)}, u32[]{:S(2)}) collective-permute-start(bf16[72,512]{1,0:T(8,128)(2,1)S(1)} %get-tuple-element.127), channel_id=1, source_target_pairs={{0,4},{1,5},{2,6},{3,7},{4,0},{5,1},{6,2},{7,3},{8,12},{9,13},{10,... | collective-permute-start | bytes 221192 | tf_op jit(solution)/shard_map/ppermute | solution.py:608
  274.7 29.2 %collective-permute-start.32 = (bf16[72,512]{1,0:T(8,128)(2,1)S(1)}, bf16[72,512]{1,0:T(8,128)(2,1)S(1)}, u32[]{:S(2)}, u32[]{:S(2)}) collective-permute-start(bf16[72,512]{1,0:T(8,128)(2,1)S(1)} %get-tuple-element.126), channel_id=1, source_target_pairs={{0,8},{1,9},{2,10},{3,11},{4,12},{5,13},{6,14},{7,15},{8,0},{9,1},... | collective-permute-start | bytes 221192 | tf_op jit(solution)/shard_map/ppermute | solution.py:608
  278.9 25.0 %collective-permute-start.33 = (bf16[72,512]{1,0:T(8,128)(2,1)S(1)}, bf16[72,512]{1,0:T(8,128)(2,1)S(1)}, u32[]{:S(2)}, u32[]{:S(2)}) collective-permute-start(bf16[72,512]{1,0:T(8,128)(2,1)S(1)} %get-tuple-element.125), channel_id=1, source_target_pairs={{0,12},{1,13},{2,14},{3,15},{4,8},{5,9},{6,10},{7,11},{8,4},{9,5},... | collective-permute-start | bytes 221192 | tf_op jit(solution)/shard_map/ppermute | solution.py:608
  321.8 49.9 %collective-permute-start.42 = (bf16[8,72,512]{2,1,0:T(8,128)(2,1)}, bf16[8,72,512]{2,1,0:T(8,128)(2,1)S(1)}, u32[]{:S(2)}, u32[]{:S(2)}) collective-permute-start(bf16[8,72,512]{2,1,0:T(8,128)(2,1)} %bitcast_dynamic-update-slice_fusion), channel_id=1, source_target_pairs={{0,1},{1,0},{2,3},{3,2},{4,5},{5,4},{6,7},{7,6},{8,9},{9,8},{10,11... | collective-permute-start | bytes 1769480 | tf_op jit(solution)/shard_map/ppermute | solution.py:608
  378.0 14.2 %collective-permute-start.43 = (bf16[512,512]{1,0:T(8,128)(2,1)S(1)}, bf16[512,512]{1,0:T(8,128)(2,1)}, u32[]{:S(2)}, u32[]{:S(2)}) collective-permute-start(bf16[512,512]{1,0:T(8,128)(2,1)S(1)} %get-tuple-element.58), channel_id=1, source_target_pairs={{0,16},{16,0},{1,17},{17,1},{2,18},{18,2},{3,19},{19,3},{4,20},{20... | collective-permute-start | bytes 1572872 | tf_op jit(solution)/shard_map/ppermute | solution.py:612
  382.9 17.4 %collective-permute-start.45 = (bf16[16,72,512]{2,1,0:T(8,128)(2,1)}, bf16[16,72,512]{2,1,0:T(8,128)(2,1)}, u32[]{:S(2)}, u32[]{:S(2)}) collective-permute-start(bf16[16,72,512]{2,1,0:T(8,128)(2,1)} %all-to-all-done.1), channel_id=1, source_target_pairs={{0,1},{1,0},{2,3},{3,2},{4,5},{5,4},{6,7},{7,6},{8,9},{9,8},{10,11... | collective-permute-start | bytes 3538952 | tf_op jit(solution)/shard_map/ppermute | solution.py:608
  404.9 12.3 %collective-permute-start.46 = (bf16[512,512]{1,0:T(8,128)(2,1)S(1)}, bf16[512,512]{1,0:T(8,128)(2,1)S(1)}, u32[]{:S(2)}, u32[]{:S(2)}) collective-permute-start(bf16[512,512]{1,0:T(8,128)(2,1)S(1)} %shard_map.316), channel_id=1, source_target_pairs={{0,16},{16,0},{1,17},{17,1},{2,18},{18,2},{3,19},{19,3},{4,20},{20... | collective-permute-start | bytes 1572872 | tf_op jit(solution)/shard_map/ppermute | solution.py:612
  430.1 25.8 %collective-permute-start.34 = (bf16[816,512]{1,0:T(8,128)(2,1)S(1)}, bf16[816,512]{1,0:T(8,128)(2,1)}, u32[]{:S(2)}, u32[]{:S(2)}) collective-permute-start(bf16[816,512]{1,0:T(8,128)(2,1)S(1)} %shard_map.313), channel_id=1, source_target_pairs={{0,16},{16,0},{1,17},{17,1},{2,18},{18,2},{3,19},{19,3},{4,20},{20... | collective-permute-start | bytes 2506760 | tf_op jit(solution)/shard_map/ppermute | solution.py:612
  431.2 20.7 %collective-permute-start.48 = (bf16[128,512]{1,0:T(8,128)(2,1)S(1)}, bf16[128,512]{1,0:T(8,128)(2,1)S(1)}, u32[]{:S(2)}, u32[]{:S(2)}) collective-permute-start(bf16[128,512]{1,0:T(8,128)(2,1)S(1)} %reduce-precision_convert_fusion.1), channel_id=1, source_target_pairs={{0,16},{16,0},{1,17},{17,1},{2,18},{18,2},{3,19},{19,3},{4,20},{20... | collective-permute-start | bytes 393224 | tf_op jit(solution)/shard_map/ppermute | solution.py:612
  (122 other events, 1317.5 us)
Sparse Core Ops, SparseCore 0:
  10.8 104.7 all-gather.6
  159.7 37.8 all-gather.10
  199.8 94.5 all-gather.8
  298.0 72.5 reduce-scatter.2
  374.8 72.6 reduce-scatter.4
  453.2 132.8 all-reduce.3

commit v2 on v0

--- a/solution.py
+++ b/solution.py
@@ -1,14 +1,983 @@
+import functools
+
 import jax
 import jax.numpy as jnp
 from jax import lax
+from jax.experimental import pallas as pl
+from jax.experimental.pallas import tpu as pltpu
 from jax.sharding import PartitionSpec as P
 
 SCALE_S = 12
 SCALE_L = 16
 SEQ_IN = 96
-
-
 EPSILON = 1e-05
+LANE = 128
+
+BF = jnp.bfloat16
+F32 = jnp.float32
+
+
+def up8(count, base=8):
+    return -(-count // base) * base
+
+
+class Plan:
+    def __init__(self, shards, length, features, down_rows, iso_rows):
+        self.shards, self.length, self.features = shards, length, features
+        self.factors = (SCALE_S, SCALE_L)
+        self.steps = tuple((length + k) // k for k in self.factors)
+        self.rows = up8(max(self.steps))
+        self.down_rows = down_rows
+        self.iso_rows = iso_rows
+        self.down_max, self.iso_max = max(down_rows), max(iso_rows)
+        self.line = shards // 4
+        self.line_taps = tuple(4 * r // features for r in down_rows)
+        blocks = features // LANE
+        self.pack = up8(max(t * blocks * n for t, n in zip(self.line_taps, self.steps)), 16)
+        self.taps = tuple(
+            max(-(-((d * r) % features + r) // features) for d in range(shards)) for r in iso_rows
+        )
+        self.taps_max = max(self.taps)
+        self.stage_rows = max(k * up8(n) for k, n in zip(self.factors, self.steps))
+
+    def mask(self, slot):
+        core, rest = divmod(slot, 2 * self.line)
+        side, line = divmod(rest, self.line)
+        return core | (side << 1) | (line << 2)
+
+
+def vmem(count):
+    return [pl.BlockSpec(memory_space=pltpu.VMEM) for _ in range(count)]
+
+
+SMEM = pl.BlockSpec(memory_space=pltpu.SMEM)
+ANY = pl.BlockSpec(memory_space=pl.ANY)
+HBM = pl.BlockSpec(memory_space=pltpu.HBM)
+
+
+def call(body, in_specs, outs, scratch, flops=0, moved=0, limit=56):
+    return pl.pallas_call(
+        body,
+        out_shape=[jax.ShapeDtypeStruct(s, d) for s, d in outs],
+        in_specs=in_specs,
+        out_specs=vmem(len(outs)),
+        scratch_shapes=scratch,
+        compiler_params=pltpu.CompilerParams(vmem_limit_bytes=limit << 20),
+        cost_estimate=pl.CostEstimate(flops=flops, bytes_accessed=moved, transcendentals=0),
+    )
+
+
+def dot(a, b, dims=((1,), (0,))):
+    return lax.dot_general(a, b, (dims, ((), ())), preferred_element_type=F32)
+
+
+def norm_parts(values):
+    center = values - jnp.mean(values, axis=-1, keepdims=True)
+    spread = jnp.mean(center * center, axis=-1, keepdims=True)
+    scale = lax.rsqrt(spread + EPSILON)
+    return center * scale, scale
+
+
+def norm_back(upstream, unit, scale, gain):
+    inner = upstream * gain
+    first = jnp.mean(inner, axis=-1, keepdims=True)
+    second = jnp.mean(inner * unit, axis=-1, keepdims=True)
+    return scale * (inner - first - unit * second)
+
+
+def keep_rows(values, count):
+    index = lax.broadcasted_iota(jnp.int32, values.shape, 0)
+    return jnp.where(index < count, values, 0.0)
+
+
+def both(meta, short, long):
+    pl.when(meta[0] == 0)(short)
+    pl.when(meta[0] == 1)(long)
+
+
+def split(rows, features):
+    return pltpu.VMEM((features // LANE, rows, LANE), F32)
+
+
+def put(ref, start, values, stride=1):
+    count = values.shape[0]
+    where = pl.ds(start, count) if stride == 1 else pl.ds(start, count, stride=stride)
+    for c in range(ref.shape[0]):
+        ref[c, where, :] = values[:, c * LANE : (c + 1) * LANE]
+
+
+def get(ref, start, count, stride=1):
+    where = pl.ds(start, count) if stride == 1 else pl.ds(start, count, stride=stride)
+    return jnp.concatenate([ref[c, where, :] for c in range(ref.shape[0])], axis=1)
+
+
+def split(rows, features):
+    return pltpu.VMEM((features // LANE, rows, LANE), F32)
+
+
+def put(ref, start, values, stride=1):
+    count = values.shape[0]
+    where = pl.ds(start, count) if stride == 1 else pl.ds(start, count, stride=stride)
+    for c in range(ref.shape[0]):
+        ref[c, where, :] = values[:, c * LANE : (c + 1) * LANE]
+
+
+def get(ref, start, count, stride=1):
+    where = pl.ds(start, count) if stride == 1 else pl.ds(start, count, stride=stride)
+    return jnp.concatenate([ref[c, where, :] for c in range(ref.shape[0])], axis=1)
+
+
+def pack_taps(plan, b, stage, first, packed):
+    k, n = plan.factors[b], plan.steps[b]
+    blocks = plan.features // LANE
+    for i in range(plan.line_taps[b]):
+        for c in range(blocks):
+            at = (i * blocks + c) * n
+            packed[at : at + n, :] = stage[c, pl.ds(first + i, n, stride=k), :]
+
+
+def unpack_taps(plan, b, packed, stage, first):
+    k, n = plan.factors[b], plan.steps[b]
+    blocks = plan.features // LANE
+    for i in range(plan.line_taps[b]):
+        for c in range(blocks):
+            at = (i * blocks + c) * n
+            stage[c, pl.ds(first + i, n, stride=k), :] = packed[at : at + n, :]
+
+
+def packed_matrix(plan, b, packed, base, matrix):
+    n = plan.steps[b]
+    for g in range(plan.line_taps[b] * plan.features // LANE):
+        matrix[base : base + n, g * LANE : (g + 1) * LANE] = packed[g * n : (g + 1) * n, :]
+
+
+def matrix_packed(plan, b, matrix, base, packed):
+    n = plan.steps[b]
+    for g in range(plan.line_taps[b] * plan.features // LANE):
+        packed[g * n : (g + 1) * n, :] = matrix[base : base + n, g * LANE : (g + 1) * LANE]
+
+
+def fetch_quarter(plan, b, meta_ref, sources, target, sems):
+    own = plan.down_rows[b]
+    quad = meta_ref[7]
+    copies = []
+    for v, source in enumerate(sources):
+        start = pl.multiple_of((quad ^ v) * own, LANE)
+        copies.append(
+            pltpu.make_async_copy(
+                source.at[pl.ds(0, own)], target.at[pl.ds(start, own)], sems.at[v]
+            )
+        )
+    for copy in copies:
+        copy.start()
+    return copies
+
+
+def total_of(parts):
+    total = parts[0][...].astype(F32)
+    for piece in parts[1:]:
+        total = total + piece[...].astype(F32)
+    return total
+
+
+def prep_blocks(plan, meta, series):
+    length, features, line = plan.length, plan.features, plan.line
+
+    def kernel(meta_ref, x_ref, out_ref, wide, packed):
+        def run(b):
+            margin = plan.factors[b] // 2
+            wide[...] = jnp.zeros_like(wide)
+            put(wide, margin, x_ref[...].astype(F32))
+            packed[...] = jnp.zeros_like(packed)
+            for z in range(line):
+                pack_taps(plan, b, wide, z * plan.line_taps[b], packed)
+                out_ref[z ^ meta_ref[5]] = packed[...].astype(BF)
+
+        both(meta_ref, lambda: run(0), lambda: run(1))
+
+    return call(
+        kernel,
+        [SMEM] + vmem(1),
+        [((line, plan.pack, LANE), BF)],
+        [split(plan.stage_rows, features), pltpu.VMEM((plan.pack, LANE), F32)],
+        moved=2 * length * features * 2,
+        limit=8,
+    )(meta, series)[0]
+
+
+def down_partial(plan, meta, blocks, quarter):
+    rows, features, line = plan.rows, plan.features, plan.line
+    wide_max = 4 * plan.down_max
+
+    def kernel(meta_ref, *refs):
+        packs, weights = refs[:line], refs[line : line + 4]
+        keep_ref, send_ref, *col_refs = refs[line + 4 : line + 10]
+        weight, wide, packed, cols, sems = refs[line + 10 :]
+
+        def run(b):
+            copies = fetch_quarter(plan, b, meta_ref, weights, weight, sems)
+            own = plan.down_rows[b]
+            wide[...] = jnp.zeros_like(wide)
+            for m in range(line):
+                packed[...] = packs[m][...].astype(F32)
+                packed_matrix(plan, b, packed, m * rows, wide)
+            matrix = wide[...].astype(BF)
+            for u in range(4):
+                piece = matrix[:, u * own : (u + 1) * own]
+                if own < plan.down_max:
+                    pad = jnp.zeros((line * rows, plan.down_max - own), BF)
+                    piece = jnp.concatenate([piece, pad], axis=1)
+                cols[u ^ meta_ref[7]] = piece
+            for v in range(4):
+                col_refs[v][...] = cols[v]
+            for copy in copies:
+                copy.wait()
+            part = dot(matrix[:, : 4 * own], weight[0 : 4 * own, :])
+            keep_ref[...] = part[:rows]
+            for m in range(1, line):
+                send_ref[m - 1] = part[m * rows : (m + 1) * rows].astype(BF)
+
+        both(meta_ref, lambda: run(0), lambda: run(1))
+
+    return call(
+        kernel,
+        [SMEM] + vmem(line) + [ANY] * 4,
+        [
+            ((rows, features), F32),
+            ((line - 1, rows, features), BF),
+        ]
+        + [((line * rows, plan.down_max), BF)] * 4,
+        [
+            pltpu.VMEM((wide_max, features), BF),
+            pltpu.VMEM((line * rows, wide_max), F32),
+            pltpu.VMEM((plan.pack, LANE), F32),
+            pltpu.VMEM((4, line * rows, plan.down_max), BF),
+            pltpu.SemaphoreType.DMA((4,)),
+        ],
+        flops=2 * line * rows * features * wide_max,
+        moved=5 << 20,
+        limit=16,
+    )(meta, *blocks, *quarter)
+
+
+def low_rows(plan, meta, pieces, biases):
+    rows, features = plan.rows, plan.features
+
+    def kernel(meta_ref, *refs):
+        parts, bias_ref, low_ref, act_ref = refs[:-3], refs[-3], refs[-2], refs[-1]
+        act = keep_rows(jnp.tanh(total_of(parts) + bias_ref[0:1, :]), meta_ref[4])
+        act_ref[...] = act
+        low_ref[...] = act.astype(BF)
+
+    return call(
+        kernel,
+        [SMEM] + vmem(len(pieces) + 1),
+        [((rows, features), BF), ((rows, features), F32)],
+        [],
+        moved=1 << 19,
+        limit=4,
+    )(meta, *pieces, biases)
+
+
+def time_major(plan, halves, stage, target, lead):
+    shards, rows = plan.shards, plan.rows
+    half = shards // 2
+    for q in range(shards):
+        put(stage, q, halves[q // half][q % half].astype(F32), shards)
+    body = shards * rows
+    if lead:
+        target[0 : lead * shards, :] = jnp.zeros((lead * shards, target.shape[1]), BF)
+    target[lead * shards : lead * shards + body, :] = get(stage, 0, body).astype(BF)
+    rest = target.shape[0] - lead * shards - body
+    if rest:
+        target[lead * shards + body :, :] = jnp.zeros((rest, target.shape[1]), BF)
+
+
+def pad_weight(plan, b, meta_ref, source, target, sem):
+    target[...] = jnp.zeros_like(target)
+    shift = pl.multiple_of(meta_ref[3], 16)
+    copy = pltpu.make_async_copy(source, target.at[pl.ds(shift, plan.iso_rows[b])], sem)
+    copy.start()
+    return copy
+
+
+def iso_partial(plan, meta, halves, w_short, w_long, backward):
+    shards, rows, features = plan.shards, plan.rows, plan.features
+    half = shards // 2
+    extra = plan.taps_max + 2
+    buffer = (max(plan.steps) + rows + extra) * shards
+
+    def kernel(
+        meta_ref, even_ref, odd_ref, ws_ref, wl_ref, keep_ref, send_ref, stage, lined, padded, sem
+    ):
+        first = meta_ref[2]
+
+        def run(b, w_ref):
+            n, taps = plan.steps[b], plan.taps[b]
+            copy = pad_weight(plan, b, meta_ref, w_ref, padded, sem)
+            lead = extra if backward else n - 1
+            time_major(plan, (even_ref, odd_ref), stage, lined, lead)
+            copy.wait()
+            for m in range(taps):
+                start = extra + n - 1 - first - m if backward else first + m
+                start = pl.multiple_of(start * shards, 16)
+                window = lined[pl.ds(start, rows * shards), :]
+                weight = padded[m * features : (m + 1) * features, :]
+                part = dot(window, weight, ((1,), (1,)) if backward else ((1,), (0,)))
+                total = part if m == 0 else total + part
+            put(stage, 0, total)
+            for q in range(shards):
+                piece = get(stage, q, rows, shards)
+                if q < half:
+                    keep_ref[q] = piece
+                else:
+                    send_ref[q - half] = piece.astype(BF)
+
+        both(meta_ref, lambda: run(0, ws_ref), lambda: run(1, wl_ref))
+
+    return call(
+        kernel,
+        [SMEM] + vmem(2) + [HBM] * 2,
+        [((half, rows, features), F32), ((half, rows, features), BF)],
+        [
+            split(rows * shards, features),
+            pltpu.VMEM((buffer, features), BF),
+            pltpu.VMEM((plan.taps_max * features, features), BF),
+            pltpu.SemaphoreType.DMA,
+        ],
+        flops=2 * shards * rows * features * features * plan.taps_max,
+        moved=10 << 20,
+        limit=56,
+    )(meta, *halves, w_short, w_long)
+
+
+def iso_weight(plan, meta, b, low_own, low_other, delta_own, delta_other):
+    shards, rows, features = plan.shards, plan.rows, plan.features
+    half = shards // 2
+    n, taps, own = plan.steps[b], plan.taps[b], plan.iso_rows[b]
+    buffer = (n - 1 + rows + taps + 1) * shards
+
+    def kernel(meta_ref, *refs):
+        lows, deltas = refs[0:4], refs[4:8]
+        grad_ref, sum_ref, stage, lined, delta, total, ordered = refs[8:]
+        me = meta_ref[1]
+
+        def load(low, steps):
+            for q in range(shards):
+                ordered[pl.ds(me ^ plan.mask(q), 1), :] = jnp.sum(
+                    steps[q // half][q % half].astype(F32), axis=0, keepdims=True
+                )
+            time_major(plan, steps, stage, delta, 0)
+            time_major(plan, low, stage, lined, n - 1)
+
+        pl.when(meta_ref[0] == b)(lambda: load(lows[0:2], deltas[0:2]))
+        pl.when(meta_ref[0] != b)(lambda: load(lows[2:4], deltas[2:4]))
+        sum_ref[...] = jnp.sum(ordered[...], axis=0, keepdims=True)
+        flat = me * own
+        first = flat // features
+        for m in range(taps):
+            start = pl.multiple_of((first + m) * shards, 16)
+            window = lined[pl.ds(start, rows * shards), :]
+            total[m * features : (m + 1) * features, :] = dot(window, delta[...], ((0,), (0,)))
+        shift = pl.multiple_of(flat % features, 16)
+        grad_ref[...] = total[pl.ds(shift, own), :]
+
+    return call(
+        kernel,
+        [SMEM] + vmem(8),
+        [((own, features), F32), ((1, features), F32)],
+        [
+            split(rows * shards, features),
+            pltpu.VMEM((buffer, features), BF),
+            pltpu.VMEM((rows * shards, features), BF),
+            pltpu.VMEM((taps * features, features), F32),
+            pltpu.VMEM((shards, features), F32),
+        ],
+        flops=2 * shards * rows * features * features * taps,
+        moved=10 << 20,
+        limit=32,
+    )(meta, *low_own, *low_other, *delta_own, *delta_other)
+
+
+def inner_rows(plan, meta, pieces, low, biases, gain):
+    rows, features = plan.rows, plan.features
+
+    def kernel(meta_ref, *refs):
+        parts = refs[:-5]
+        low_ref, bias_ref, gain_ref, inner_ref, act_ref = refs[-5:]
+        act = jnp.tanh(total_of(parts) + bias_ref[1:2, :])
+        act_ref[...] = act
+        unit, _ = norm_parts(act + low_ref[...].astype(F32))
+        inner = unit * gain_ref[...] + bias_ref[3:4, :]
+        inner_ref[...] = keep_rows(inner, meta_ref[4]).astype(BF)
+
+    return call(
+        kernel,
+        [SMEM] + vmem(len(pieces) + 3),
+        [((rows, features), BF), ((rows, features), F32)],
+        [],
+        moved=1 << 19,
+        limit=4,
+    )(meta, *pieces, low, biases, gain)
+
+
+def trans_forward(plan, meta, inners, quarter):
+    rows, features, line = plan.rows, plan.features, plan.line
+    wide_max = 4 * plan.down_max
+
+    def kernel(meta_ref, *refs):
+        inner_refs, weights = refs[:line], refs[line : line + 4]
+        out_ref, weight, wide, packed, sems = refs[line + 4 :]
+
+        def run(b):
+            copies = fetch_quarter(plan, b, meta_ref, weights, weight, sems)
+            lhs = jnp.concatenate([ref[...] for ref in inner_refs], axis=0)
+            for copy in copies:
+                copy.wait()
+            for i in range(plan.line_taps[b]):
+                wide[:, i * features : (i + 1) * features] = dot(
+                    lhs, weight[i * features : (i + 1) * features, :]
+                )
+            packed[...] = jnp.zeros_like(packed)
+            for m in range(line):
+                matrix_packed(plan, b, wide, m * rows, packed)
+                out_ref[m] = packed[...].astype(BF)
+
+        both(meta_ref, lambda: run(0), lambda: run(1))
+
+    return call(
+        kernel,
+        [SMEM] + vmem(line) + [ANY] * 4,
+        [((line, plan.pack, LANE), BF)],
+        [
+            pltpu.VMEM((wide_max, features), BF),
+            pltpu.VMEM((line * rows, wide_max), F32),
+            pltpu.VMEM((plan.pack, LANE), F32),
+            pltpu.SemaphoreType.DMA((4,)),
+        ],
+        flops=2 * line * rows * features * wide_max,
+        moved=4 << 20,
+        limit=16,
+    )(meta, *inners, *quarter)[0]
+
+
+def outer_rows(plan, meta, packs, series, biases, gain):
+    features, length, line = plan.features, plan.length, plan.line
+    half_rows = length // 2
+
+    def kernel(meta_ref, *refs):
+        pack_refs = refs[:line]
+        x_ref, bias_ref, gain_ref, keep_ref, send_ref, act_ref, stage, packed = refs[line:]
+
+        def run(b):
+            for m in range(line):
+                packed[...] = pack_refs[m][...].astype(F32)
+                unpack_taps(plan, b, packed, stage, (meta_ref[5] ^ m) * plan.line_taps[b])
+
+        both(meta_ref, lambda: run(0), lambda: run(1))
+        act = jnp.tanh(get(stage, 0, length) + bias_ref[2:3, :])
+        act_ref[...] = act
+        unit, _ = norm_parts(act + x_ref[...].astype(F32))
+        put(stage, 0, unit * gain_ref[...] + bias_ref[3:4, :])
+        mine = pl.multiple_of(meta_ref[0] * half_rows, 8)
+        other = pl.multiple_of((1 - meta_ref[0]) * half_rows, 8)
+        keep_ref[...] = get(stage, mine, half_rows).astype(BF)
+        send_ref[...] = get(stage, other, half_rows).astype(BF)
+
+    return call(
+        kernel,
+        [SMEM] + vmem(line + 3),
+        [((half_rows, features), BF), ((half_rows, features), BF), ((length, features), F32)],
+        [split(plan.stage_rows, features), pltpu.VMEM((plan.pack, LANE), F32)],
+        moved=6 << 20,
+        limit=16,
+    )(meta, *packs, series, biases, gain)
+
+
+def outer_backward(plan, meta, up_keep, up_recv, series, act, gain):
+    features, length, line = plan.features, plan.length, plan.line
+    half_rows = length // 2
+
+    def kernel(
+        meta_ref, uk_ref, ur_ref, x_ref, act_ref, gain_ref,
+        outer_ref, taps_ref, vec_ref, stage, upstream, packed,
+    ):
+        mine = pl.multiple_of(meta_ref[0] * half_rows, 8)
+        other = pl.multiple_of((1 - meta_ref[0]) * half_rows, 8)
+        upstream[pl.ds(mine, half_rows), :] = uk_ref[...].astype(F32)
+        upstream[pl.ds(other, half_rows), :] = ur_ref[...].astype(F32)
+        act_value = act_ref[...]
+        unit, scale = norm_parts(act_value + x_ref[...].astype(F32))
+        above = upstream[...]
+        vec_ref[...] = jnp.zeros_like(vec_ref)
+        vec_ref[1:2, :] = jnp.sum(above, axis=0, keepdims=True)
+        vec_ref[2:3, :] = jnp.sum(above * unit, axis=0, keepdims=True)
+        outer = norm_back(above, unit, scale, gain_ref[...])
+        outer_ref[...] = outer
+        delta = (outer * (1.0 - act_value * act_value)).astype(BF).astype(F32)
+        vec_ref[0:1, :] = jnp.sum(delta, axis=0, keepdims=True)
+        put(stage, 0, delta)
+        put(stage, length, jnp.zeros((plan.stage_rows - length, features), F32))
+        packed[...] = jnp.zeros_like(packed)
+
+        def run(b):
+            for m in range(line):
+                pack_taps(plan, b, stage, (meta_ref[5] ^ m) * plan.line_taps[b], packed)
+                taps_ref[m] = packed[...].astype(BF)
+
+        both(meta_ref, lambda: run(0), lambda: run(1))
+
+    return call(
+        kernel,
+        [SMEM] + vmem(5),
+        [((length, features), F32), ((line, plan.pack, LANE), BF), ((8, features), F32)],
+        [
+            split(plan.stage_rows, features),
+            pltpu.VMEM((length, features), F32),
+            pltpu.VMEM((plan.pack, LANE), F32),
+        ],
+        moved=8 << 20,
+        limit=20,
+    )(meta, up_keep, up_recv, series, act, gain)
+
+
+def trans_backward(plan, meta, packs, quarter):
+    rows, features, line = plan.rows, plan.features, plan.line
+    wide_max = 4 * plan.down_max
+
+    def kernel(meta_ref, *refs):
+        pack_refs, weights = refs[:line], refs[line : line + 4]
+        keep_ref, send_ref, wide_ref, weight, wide, packed, sems = refs[line + 4 :]
+
+        def run(b):
+            copies = fetch_quarter(plan, b, meta_ref, weights, weight, sems)
+            wide[...] = jnp.zeros_like(wide)
+            for m in range(line):
+                packed[...] = pack_refs[m][...].astype(F32)
+                packed_matrix(plan, b, packed, m * rows, wide)
+            matrix = wide[...].astype(BF)
+            wide_ref[...] = matrix
+            for copy in copies:
+                copy.wait()
+            for i in range(plan.line_taps[b]):
+                part = dot(
+                    matrix[:, i * features : (i + 1) * features],
+                    weight[i * features : (i + 1) * features, :],
+                    ((1,), (1,)),
+                )
+                total = part if i == 0 else total + part
+            keep_ref[...] = total[:rows]
+            for m in range(1, line):
+                send_ref[m - 1] = total[m * rows : (m + 1) * rows].astype(BF)
+
+        both(meta_ref, lambda: run(0), lambda: run(1))
+
+    return call(
+        kernel,
+        [SMEM] + vmem(line) + [ANY] * 4,
+        [
+            ((rows, features), F32),
+            ((line - 1, rows, features), BF),
+            ((line * rows, wide_max), BF),
+        ],
+        [
+            pltpu.VMEM((wide_max, features), BF),
+            pltpu.VMEM((line * rows, wide_max), F32),
+            pltpu.VMEM((plan.pack, LANE), F32),
+            pltpu.SemaphoreType.DMA((4,)),
+        ],
+        flops=2 * line * rows * features * wide_max,
+        moved=5 << 20,
+        limit=16,
+    )(meta, *packs, *quarter)
+
+
+def trans_weight(plan, meta, inners, wide):
+    rows, features, line = plan.rows, plan.features, plan.line
+    most = plan.down_max
+
+    def kernel(meta_ref, *refs):
+        inner_refs = refs[:line]
+        wide_ref, keep_ref, send_ref, total = refs[line:]
+
+        def run(b):
+            own = plan.down_rows[b]
+            lhs = jnp.concatenate([ref[...] for ref in inner_refs], axis=0)
+            for i in range(plan.line_taps[b]):
+                total[i * features : (i + 1) * features, :] = dot(
+                    lhs, wide_ref[:, i * features : (i + 1) * features], ((0,), (0,))
+                )
+            for v in range(4):
+                start = pl.multiple_of((meta_ref[7] ^ v) * own, LANE)
+                piece = total[pl.ds(start, own), :]
+                if own < most:
+                    pad = jnp.zeros((most - own, features), F32)
+                    piece = jnp.concatenate([piece, pad], axis=0)
+                if v % 2 == 0:
+                    keep_ref[v // 2] = piece
+                else:
+                    send_ref[v // 2] = piece.astype(BF)
+
+        both(meta_ref, lambda: run(0), lambda: run(1))
+
+    return call(
+        kernel,
+        [SMEM] + vmem(line + 1),
+        [((2, most, features), F32), ((2, most, features), BF)],
+        [pltpu.VMEM((4 * most, features), F32)],
+        flops=2 * line * rows * features * 4 * most,
+        moved=5 << 20,
+        limit=20,
+    )(meta, *inners, wide)
+
+
+def inner_backward(plan, meta, pieces, low, act, vectors, gain):
+    rows, features = plan.rows, plan.features
+
+    def kernel(meta_ref, *refs):
+        parts = refs[:-7]
+        low_ref, act_ref, vec_ref, gain_ref, delta_ref, back_ref, out_ref = refs[-7:]
+        total = keep_rows(total_of(parts), meta_ref[4])
+        act_in = act_ref[...]
+        unit, scale = norm_parts(act_in + low_ref[...].astype(F32))
+        out_ref[...] = vec_ref[...]
+        out_ref[1:2, :] = vec_ref[1:2, :] + jnp.sum(total, axis=0, keepdims=True)
+        out_ref[2:3, :] = vec_ref[2:3, :] + jnp.sum(total * unit, axis=0, keepdims=True)
+        back = norm_back(total, unit, scale, gain_ref[...])
+        back_ref[...] = back
+        delta_ref[...] = keep_rows(back * (1.0 - act_in * act_in), meta_ref[4]).astype(BF)
+
+    return call(
+        kernel,
+        [SMEM] + vmem(len(pieces) + 4),
+        [((rows, features), BF), ((rows, features), F32), ((8, features), F32)],
+        [],
+        moved=1 << 19,
+        limit=6,
+    )(meta, *pieces, low, act, vectors, gain)
+
+
+def down_delta(plan, meta, pieces, delta_inner, act, small):
+    rows, features = plan.rows, plan.features
+    base, extra = up8(rows, 16), small.shape[0]
+
+    def kernel(meta_ref, *refs):
+        parts = refs[:-4]
+        inner_ref, act_ref, small_ref, out_ref = refs[-4:]
+        value = act_ref[...]
+        total = total_of(parts) + inner_ref[...]
+        delta = keep_rows(total * (1.0 - value * value), meta_ref[4])
+        pad = jnp.zeros((base - rows, features), F32)
+        out_ref[0:base, :] = jnp.concatenate([delta, pad], axis=0).astype(BF)
+        high = small_ref[...].astype(BF)
+        out_ref[base : base + extra, :] = high
+        out_ref[base + extra :, :] = (small_ref[...] - high.astype(F32)).astype(BF)
+
+    return call(
+        kernel,
+        [SMEM] + vmem(len(pieces) + 3),
+        [((base + 2 * extra, features), BF)],
+        [],
+        moved=1 << 19,
+        limit=8,
+    )(meta, *pieces, delta_inner, act, small)[0]
+
+
+def input_quarter(plan, meta, deltas, quarter):
+    features, line = plan.features, plan.line
+    rows = up8(plan.rows, 16)
+    wide_max = 4 * plan.down_max
+
+    def kernel(meta_ref, *refs):
+        delta_refs, weights = refs[:line], refs[line : line + 4]
+        out_ref, weight, wide, packed, sems = refs[line + 4 :]
+
+        def run(b):
+            copies = fetch_quarter(plan, b, meta_ref, weights, weight, sems)
+            lhs = jnp.concatenate([ref[0:rows, :] for ref in delta_refs], axis=0)
+            for copy in copies:
+                copy.wait()
+            for i in range(plan.line_taps[b]):
+                wide[:, i * features : (i + 1) * features] = dot(
+                    lhs, weight[i * features : (i + 1) * features, :], ((1,), (1,))
+                )
+            packed[...] = jnp.zeros_like(packed)
+            for m in range(line):
+                matrix_packed(plan, b, wide, m * rows, packed)
+                out_ref[m] = packed[...].astype(BF)
+
+        both(meta_ref, lambda: run(0), lambda: run(1))
+
+    return call(
+        kernel,
+        [SMEM] + vmem(line) + [ANY] * 4,
+        [((line, plan.pack, LANE), BF)],
+        [
+            pltpu.VMEM((wide_max, features), BF),
+            pltpu.VMEM((line * rows, wide_max), F32),
+            pltpu.VMEM((plan.pack, LANE), F32),
+            pltpu.SemaphoreType.DMA((4,)),
+        ],
+        flops=2 * line * rows * features * wide_max,
+        moved=4 << 20,
+        limit=16,
+    )(meta, *deltas, *quarter)[0]
+
+
+def input_rows(plan, meta, packs, outer):
+    features, length, line = plan.features, plan.length, plan.line
+
+    def kernel(meta_ref, *refs):
+        pack_refs = refs[:line]
+        outer_ref, out_ref, stage, packed = refs[line:]
+
+        def run(b):
+            for m in range(line):
+                packed[...] = pack_refs[m][...].astype(F32)
+                unpack_taps(plan, b, packed, stage, (meta_ref[5] ^ m) * plan.line_taps[b])
+            inner = get(stage, plan.factors[b] // 2, length)
+            out_ref[...] = (inner + outer_ref[...]).astype(BF)
+
+        both(meta_ref, lambda: run(0), lambda: run(1))
+
+    return call(
+        kernel,
+        [SMEM] + vmem(line + 1),
+        [((length, features), BF)],
+        [split(plan.stage_rows, features), pltpu.VMEM((plan.pack, LANE), F32)],
+        moved=3 << 20,
+        limit=12,
+    )(meta, *packs, outer)[0]
+
+
+def down_weight(plan, meta, columns, even, odd, extra):
+    shards, rows, features, line = plan.shards, plan.rows, plan.features, plan.line
+    half = shards // 2
+    base = up8(rows, 16)
+
+    def kernel(meta_ref, *refs):
+        col_refs = refs[:4]
+        even_ref, odd_ref, grad_ref, sum_ref, small_ref, delta, ordered, small = refs[4:]
+        me = meta_ref[1]
+        for q in range(shards):
+            source = (even_ref, odd_ref)[q // half]
+            value = source[q % half, 0:base, :].astype(F32)
+            at = me ^ plan.mask(q)
+            ordered[pl.ds(at, 1), :] = jnp.sum(value, axis=0, keepdims=True)
+            delta[q * rows : (q + 1) * rows, :] = value[:rows]
+            high = source[q % half, base : base + extra, :].astype(F32)
+            low = source[q % half, base + extra : base + 2 * extra, :].astype(F32)
+            small[at] = high + low
+        sum_ref[...] = jnp.sum(ordered[...], axis=0, keepdims=True)
+        total = small[0]
+        for i in range(1, shards):
+            total = total + small[i]
+        small_ref[...] = total
+        for at, v in enumerate((0, 2, 1, 3)):
+            steps = delta[at * line * rows : (at + 1) * line * rows, :].astype(BF)
+            part = dot(col_refs[v][...], steps, ((0,), (0,)))
+            total = part if at == 0 else total + part
+        grad_ref[...] = total.astype(BF)
+
+    return call(
+        kernel,
+        [SMEM] + vmem(6),
+        [((plan.down_max, features), BF), ((1, features), F32), ((extra, features), F32)],
+        [
+            pltpu.VMEM((shards * rows, features), F32),
+            pltpu.VMEM((shards, features), F32),
+            pltpu.VMEM((shards, extra, features), F32),
+        ],
+        flops=2 * shards * rows * features * features,
+        moved=4 << 20,
+        limit=20,
+    )(meta, *columns, even, odd)
+
+
+ROOT_HALF = 0.7071067811865476
+ROOT_TWO_PI = 0.3989422804014327
+
+
+def head_rows(plan, meta, keep, recv, target, valid, merge, bias, gain, ff_in, ff_bias, ff_out):
+    half_rows, features = keep.shape
+    hidden = ff_in.shape[1]
+    parts = hidden // features
+    dims = (half_rows, features)
+
+    def kernel(
+        meta_ref, keep_ref, recv_ref, target_ref, valid_ref, merge_ref, bias_ref, gain_ref,
+        in_bias_ref, in_hbm, out_hbm,
+        out_ref, up_keep_ref, up_send_ref, normed_ref, act_ref, pre_delta_ref, ff_delta_ref,
+        merged_delta_ref, vec_ref, loss_ref, slope_ref, in_ref, out_w_ref, sems,
+    ):
+        fetch_in = pltpu.make_async_copy(in_hbm, in_ref, sems.at[0])
+        fetch_out = pltpu.make_async_copy(out_hbm, out_w_ref, sems.at[1])
+        fetch_in.start()
+        fetch_out.start()
+        branch = meta_ref[0]
+        merged = dot(keep_ref[...], merge_ref[branch]) + dot(recv_ref[...], merge_ref[1 - branch])
+        merged = merged + bias_ref[0:1, :]
+        unit, scale = norm_parts(merged)
+        normed = (unit * gain_ref[0:1, :] + bias_ref[2:3, :]).astype(BF)
+        normed_ref[...] = normed
+        fetch_in.wait()
+        fetch_out.wait()
+        for c in range(parts):
+            cols = slice(c * features, (c + 1) * features)
+            pre = dot(normed, in_ref[:, cols]) + in_bias_ref[:, cols]
+            share = 0.5 * (1.0 + lax.erf(pre * ROOT_HALF))
+            slope_ref[:, cols] = share + pre * (jnp.exp(-0.5 * pre * pre) * ROOT_TWO_PI)
+            act = (pre * share).astype(BF)
+            act_ref[:, cols] = act
+            part = dot(act, out_w_ref[cols, :])
+            total = part if c == 0 else total + part
+        unit_end, scale_end = norm_parts(merged + total + bias_ref[1:2, :])
+        final = unit_end * gain_ref[1:2, :] + bias_ref[3:4, :]
+        out_ref[...] = final.astype(BF)
+        error = final - target_ref[...].astype(F32)
+        weighted = valid_ref[...] * error
+        loss = jnp.sum(jnp.sum(weighted * error, axis=0, keepdims=True), axis=1, keepdims=True)
+        loss_ref[...] = jnp.broadcast_to(loss, loss_ref.shape)
+        vec_ref[...] = jnp.zeros_like(vec_ref)
+        vec_ref[3:4, :] = jnp.sum(weighted, axis=0, keepdims=True)
+        vec_ref[5:6, :] = jnp.sum(weighted * unit_end, axis=0, keepdims=True)
+        delta_sum = norm_back(weighted, unit_end, scale_end, gain_ref[1:2, :])
+        delta_ff = delta_sum.astype(BF)
+        ff_delta_ref[...] = delta_ff
+        vec_ref[1:2, :] = jnp.sum(delta_ff.astype(F32), axis=0, keepdims=True)
+        for c in range(parts):
+            cols = slice(c * features, (c + 1) * features)
+            pre_delta = dot(delta_ff, out_w_ref[cols, :], ((1,), (1,))) * slope_ref[:, cols]
+            pre_delta = pre_delta.astype(BF)
+            pre_delta_ref[:, cols] = pre_delta
+            vec_ref[6 + c : 7 + c, :] = jnp.sum(pre_delta.astype(F32), axis=0, keepdims=True)
+            part = dot(pre_delta, in_ref[:, cols], ((1,), (1,)))
+            above = part if c == 0 else above + part
+        vec_ref[2:3, :] = jnp.sum(above, axis=0, keepdims=True)
+        vec_ref[4:5, :] = jnp.sum(above * unit, axis=0, keepdims=True)
+        delta = norm_back(above, unit, scale, gain_ref[0:1, :]) + delta_sum
+        delta = delta.astype(BF)
+        merged_delta_ref[...] = delta
+        vec_ref[0:1, :] = jnp.sum(delta.astype(F32), axis=0, keepdims=True)
+        up_keep_ref[...] = dot(delta, merge_ref[branch], ((1,), (1,))).astype(BF)
+        up_send_ref[...] = dot(delta, merge_ref[1 - branch], ((1,), (1,))).astype(BF)
+
+    vec_rows = up8(6 + parts + 6)
+    return call(
+        kernel,
+        [SMEM] + vmem(8) + [HBM] * 2,
+        [
+            (dims, BF), (dims, BF), (dims, BF), (dims, BF),
+            ((half_rows, hidden), BF), ((half_rows, hidden), BF), (dims, BF), (dims, BF),
+            ((vec_rows, features), F32), ((8, LANE), F32),
+        ],
+        [
+            pltpu.VMEM((half_rows, hidden), F32),
+            pltpu.VMEM((features, hidden), BF),
+            pltpu.VMEM((hidden, features), BF),
+            pltpu.SemaphoreType.DMA((2,)),
+        ],
+        flops=10 * half_rows * features * hidden,
+        moved=14 << 20,
+        limit=56,
+    )(meta, keep, recv, target, valid, merge, bias, gain, ff_bias, ff_in, ff_out)
+
+
+def head_weights(plan, meta, keep, recv, normed, act, pre_delta, ff_delta, merged_delta):
+    shards = plan.shards
+    half_rows, features = keep.shape
+    hidden = act.shape[1]
+    ff_rows, merge_rows = hidden // shards // 2, features // shards
+    parts, half = hidden // features, shards // 2
+    own = 2 * ff_rows + merge_rows
+
+    def kernel(
+        meta_ref, keep_ref, recv_ref, normed_ref, act_ref, pre_ref, ff_ref, merged_ref,
+        stay_ref, send_ref, first, second, third,
+    ):
+        branch = meta_ref[0]
+        for c in range(parts):
+            cols = slice(c * features, (c + 1) * features)
+            first[cols, :] = dot(pre_ref[:, cols], normed_ref[...], ((0,), (0,))).astype(BF)
+            second[cols, :] = dot(act_ref[:, cols], ff_ref[...], ((0,), (0,))).astype(BF)
+        for side, ref in enumerate((keep_ref, recv_ref)):
+            part = dot(ref[...], merged_ref[...], ((0,), (0,))).astype(BF)
+            start = pl.multiple_of((branch ^ side) * features, 16)
+            third[pl.ds(start, features), :] = part
+        for q in range(shards):
+            device = meta_ref[1] ^ plan.mask(q)
+            target = stay_ref if q < half else send_ref
+            for h in range(2):
+                at = 2 * device + (branch ^ h)
+                for start, count, source in (
+                    (0, ff_rows, first),
+                    (ff_rows, ff_rows, second),
+                    (2 * ff_rows, merge_rows, third),
+                ):
+                    rows = pl.ds(pl.multiple_of(at * count, 16), count)
+                    target[h, q % half, start : start + count, :] = source[rows, :]
+
+    return call(
+        kernel,
+        [SMEM] + vmem(7),
+        [((2, half, own, features), BF), ((2, half, own, features), BF)],
+        [
+            pltpu.VMEM((hidden, features), BF),
+            pltpu.VMEM((hidden, features), BF),
+            pltpu.VMEM((2 * features, features), BF),
+        ],
+        flops=4 * half_rows * features * hidden,
+        moved=12 << 20,
+        limit=24,
+    )(meta, keep, recv, normed, act, pre_delta, ff_delta, merged_delta)
+
+
+def hop(values, distance, shards):
+    return lax.ppermute(values, "series", [(i, i ^ distance) for i in range(shards)])
+
+
+def swap(values):
+    return lax.ppermute(values, "branch", [(0, 1), (1, 0)])
+
+
+def after(value, *others):
+    return lax.optimization_barrier((value, others))[0]
+
+
+def along_line(plan, own):
+    return [own] + [hop(own, i << 2, plan.shards) for i in range(1, plan.line)]
+
+
+def line_parts(plan, first, rest):
+    return [first] + [hop(rest[i - 1], i << 2, plan.shards) for i in range(1, plan.line)]
+
+
+def quad_gather(plan, own, later):
+    side = hop(own, 2, plan.shards)
+    return [own, hop(own, 1, plan.shards), side, hop(after(side, later), 1, plan.shards)]
+
+
+def settle(value, *others):
+    return lax.optimization_barrier((value,) + others)
+
+
+def gather_slots(plan, line):
+    even = jnp.stack(line + [hop(value, 2, plan.shards) for value in line])
+    return even, hop(even, 1, plan.shards)
+
+
+def scatter_sum(plan, keep, send, *others):
+    shards, line = plan.shards, plan.line
+    first = keep + hop(send, 1, shards).astype(F32)
+    second = first[:line] + hop(first[line:].astype(BF), 2, shards).astype(F32)
+    if others:
+        second, *others = settle(second, *others)
+    pieces = line_parts(plan, second[0], [second[i].astype(BF) for i in range(1, line)])
+    return (pieces, *others) if others else pieces
+
+
+def rounded(values):
+    return lax.reduce_precision(values, exponent_bits=8, mantissa_bits=7)
 
 
 def layer_norm(values, gain_row, shift_row):
@@ -21,19 +990,226 @@
     return jax.nn.gelu(values, approximate=False)
 
 
-def product(first_operand, second_operand):
-    return jnp.dot(first_operand, second_operand, preferred_element_type=jnp.float32)
-
-
-def left_product(first_operand, second_operand):
-    return jnp.einsum(
-        "mi,mo->io", first_operand, second_operand, preferred_element_type=jnp.float32
-    )
-
-
-def right_product(first_operand, second_operand):
-    return jnp.einsum(
-        "mo,io->mi", first_operand, second_operand, preferred_element_type=jnp.float32
+def product(a, b):
+    return jnp.dot(a, b, preferred_element_type=F32)
+
+
+def left_product(a, b):
+    return jnp.einsum("mi,mo->io", a, b, preferred_element_type=F32)
+
+
+def right_product(a, b):
+    return jnp.einsum("mo,io->mi", a, b, preferred_element_type=F32)
+
+
+def body(
+    series_in, target, horizons, observed,
+    down_short, iso_short, trans_short, down_long, iso_long, trans_long,
+    branch_bias, branch_gain, merge_weight, head_bias, head_gain, ff_in, ff_in_bias, ff_out,
+):
+    shards = lax.axis_size("series")
+    _, length, features = series_in.shape
+    plan = Plan(
+        shards,
+        length,
+        features,
+        (down_short.shape[0], down_long.shape[0]),
+        (iso_short.shape[0], iso_long.shape[0]),
+    )
+    line = plan.line
+    half_rows = length // 2
+    branch = lax.axis_index("branch")
+    me = lax.axis_index("series")
+    is_short = branch == 0
+    iso_rows = jnp.where(is_short, plan.iso_rows[0], plan.iso_rows[1])
+    meta = jnp.stack(
+        [
+            branch,
+            me,
+            (me * iso_rows) // features,
+            (me * iso_rows) % features,
+            jnp.where(is_short, plan.steps[0], plan.steps[1]),
+            me // 4,
+            me % 2,
+            me % 4,
+        ]
+    ).astype(jnp.int32)
+    series = series_in[0]
+    biases, gain = branch_bias[0], branch_gain
+
+    def chosen(short, long):
+        rows = max(short.shape[0], long.shape[0])
+        short = jnp.pad(short, ((0, rows - short.shape[0]), (0, 0)))
+        long = jnp.pad(long, ((0, rows - long.shape[0]), (0, 0)))
+        return jnp.where(is_short, short, long)
+
+    blocks = prep_blocks(plan, meta, series)
+    own_down = after(chosen(down_short, down_long), blocks)
+    blocks = line_parts(plan, blocks[0], [blocks[i] for i in range(1, line)])
+    down_quarter = quad_gather(plan, own_down, blocks)
+    own_trans = after(chosen(trans_short, trans_long), blocks)
+    keep, send, *columns = down_partial(plan, meta, blocks, down_quarter)
+    pieces = line_parts(plan, keep, send)
+    trans_quarter = quad_gather(plan, own_trans, pieces)
+    low, act_down = low_rows(plan, meta, pieces, biases)
+    low_own = gather_slots(plan, along_line(plan, low))
+    low_own, trans_quarter = settle(low_own, trans_quarter)
+    keep, send = iso_partial(plan, meta, low_own, iso_short, iso_long, False)
+    low_other = swap(after(low_own[0], low_own[1]))
+    pieces = scatter_sum(plan, keep, send)
+    inner, act_iso = inner_rows(plan, meta, pieces, low, biases, gain)
+    columns[2] = hop(after(columns[2], inner), 2, shards)
+    inners, columns = settle(along_line(plan, inner), columns)
+    packs = trans_forward(plan, meta, inners, trans_quarter)
+    columns[3] = hop(after(columns[3], packs), 3, shards)
+    packs = line_parts(plan, packs[0], [packs[i] for i in range(1, line)])
+    packs, columns, low_other = settle(packs, columns, low_other)
+    out_keep, out_send, act_trans = outer_rows(plan, meta, packs, series, biases, gain)
+    out_recv = swap(out_send)
+    columns[1] = hop(after(columns[1], out_keep), 1, shards)
+    low_other = (low_other, hop(after(low_other, out_keep), 1, shards))
+    out_recv, columns, low_other = settle(out_recv, columns, low_other)
+
+    positions = branch * half_rows + jnp.arange(half_rows, dtype=jnp.int32)
+    observed_half = lax.dynamic_slice_in_dim(observed[0], branch * half_rows, half_rows, 0)
+    valid = (
+        observed_half.astype(F32)
+        * (positions >= SEQ_IN).astype(F32)
+        * (positions < SEQ_IN + horizons[0]).astype(F32)
+    )
+    (
+        out, up_keep, up_send, normed, act_ff, pre_delta, ff_delta, merged_delta, vec_head, loss_part
+    ) = head_rows(
+        plan, meta, out_keep, out_recv, target[0], valid[:, None], merge_weight, head_bias,
+        head_gain, ff_in, ff_in_bias[None], ff_out,
+    )
+    up_recv = swap(up_send)
+    shares, share_send = head_weights(
+        plan, meta, out_keep, out_recv, normed, act_ff, pre_delta, ff_delta, merged_delta
+    )
+
+    outer, packs, vectors = outer_backward(plan, meta, up_keep, up_recv, series, act_trans, gain)
+    share_recv = hop(after(share_send, packs), 1, shards)
+    shares = shares.astype(F32) + share_recv.astype(F32)
+    share_recv = hop(shares[:, line:].astype(BF), 2, shards)
+    packs = line_parts(plan, packs[0], [packs[i] for i in range(1, line)])
+    keep, send, wide = trans_backward(plan, meta, packs, trans_quarter)
+    trans_keep, trans_send = trans_weight(plan, meta, inners, wide)
+    pieces, trans_send, share_recv = settle(line_parts(plan, keep, send), trans_send, share_recv)
+    shares = shares[:, :line] + share_recv.astype(F32)
+    share_recv = swap(shares[1].astype(BF))
+    shares = shares[0]
+    delta_iso, delta_inner, vectors = inner_backward(
+        plan, meta, pieces, low, act_iso, vectors, gain
+    )
+    ff_parts = ff_in_bias.shape[0] // features
+    selector = jnp.stack([is_short, branch == 1]).astype(F32)
+    branch_rows = (selector[:, None, None] * vectors[None, 0:3]).reshape(6, features)
+    small = jnp.concatenate([vec_head[: 6 + ff_parts], branch_rows], axis=0)
+    count = small.shape[0]
+    small = jnp.pad(small, ((0, up8(count, 16) - count), (0, 0)))
+    trans_recv = hop(trans_send, 1, shards)
+    deltas, trans_recv = settle(along_line(plan, delta_iso), trans_recv)
+    trans_sum = trans_keep + trans_recv.astype(F32)
+    trans_next = trans_sum[1].astype(BF)
+    delta_own = gather_slots(plan, deltas)
+    delta_own, trans_next, share_recv = settle(delta_own, trans_next, share_recv)
+    shares = shares + share_recv.astype(F32)
+    spread = line // 2
+    share_recv = hop(shares[spread:].astype(BF), 4 * spread, shards)
+    keep, send = iso_partial(plan, meta, delta_own, iso_short, iso_long, True)
+    delta_other = swap(delta_own[0])
+    pieces, delta_other, share_recv = scatter_sum(plan, keep, send, delta_other, share_recv)
+    delta_other = (delta_other, hop(delta_other, 1, shards))
+    pieces, delta_other = settle(pieces, delta_other)
+    shares = shares[:spread] + share_recv.astype(F32)
+    payload = down_delta(plan, meta, pieces, delta_inner, act_down, small)
+    first_grad = iso_weight(
+        plan, meta, 0, after(low_own, payload), low_other, delta_own, delta_other
+    )
+    trans_recv = hop(after(trans_next, payload), 2, shards)
+    share_recv = hop(after(shares[1:].astype(BF), payload), 4, shards)
+    deltas, trans_recv, share_recv, first_grad = settle(
+        along_line(plan, payload), trans_recv, share_recv, first_grad
+    )
+    shares = rounded(shares[0] + share_recv[0].astype(F32))
+    grad_trans = (trans_sum[0] + trans_recv.astype(F32)).astype(BF)
+    share_recv = swap(shares.astype(BF))
+    packs = input_quarter(plan, meta, deltas, down_quarter)
+    even = jnp.stack(deltas)
+    odd = hop(after(even, packs), 2, shards)
+    packs = line_parts(plan, packs[0], [packs[i] for i in range(1, line)])
+    trans_recv = swap(grad_trans)
+    packs, odd, share_recv, trans_recv = settle(packs, odd, share_recv, trans_recv)
+    share_recv = share_recv.astype(F32)
+    ff_rows = ff_in_bias.shape[0] // shards // 2
+    halves = [
+        jnp.where(is_short, shares, share_recv),
+        jnp.where(is_short, share_recv, shares),
+    ]
+    merge_own = jnp.concatenate([half[2 * ff_rows :] for half in halves], axis=0)
+    merge_all = lax.all_gather(merge_own.astype(BF), "series", axis=0)
+    even = jnp.concatenate([even, odd], axis=0)
+    delta_halves = (even, hop(even, 1, shards))
+    input_own = input_rows(plan, meta, packs, outer)
+    input_recv = swap(input_own)
+    grad_down, down_sum, small = down_weight(
+        plan, meta, columns, *after(delta_halves, input_own), small.shape[0]
+    )
+    down_recv = swap(grad_down)
+    loss_row = jnp.broadcast_to(loss_part[0:1, 0:1], (1, features))
+    mine = jnp.concatenate([small[:count], down_sum, loss_row], axis=0)
+    theirs = swap(mine)
+    second_grad = iso_weight(
+        plan, meta, 1, after(low_own, grad_down), low_other, delta_own, delta_other
+    )
+    input_recv = after(input_recv, second_grad)
+    iso_grads = [first_grad, second_grad]
+
+    def placed(own, other, b, rows):
+        return jnp.where(branch == b, own, other)[:rows].astype(F32)
+
+    merge_total = merge_all.astype(F32).reshape(2, features, features)
+    both_sums = mine + theirs
+    loss = (0.5 / (features * length)) * both_sums[count + 1, 0:1]
+    small = both_sums[:count]
+    down_sum, down_other = mine[count : count + 1], theirs[count : count + 1]
+    branch_total = small[6 + ff_parts :].reshape(2, 3, features)
+    down_sums = jnp.stack(
+        [jnp.where(is_short, down_sum, down_other), jnp.where(is_short, down_other, down_sum)]
+    )
+    iso_sums = jnp.stack([iso_grads[0][1], iso_grads[1][1]])
+    bias_total = jnp.concatenate([down_sums, iso_sums, branch_total[:, 0:2]], axis=1)
+
+    others = (
+        iso_grads[0][0],
+        placed(grad_trans, trans_recv, 0, plan.down_rows[0]),
+        iso_grads[1][0],
+        placed(grad_trans, trans_recv, 1, plan.down_rows[1]),
+        merge_total,
+        jnp.concatenate([half[:ff_rows] for half in halves], axis=0).T,
+        jnp.concatenate([half[ff_rows : 2 * ff_rows] for half in halves], axis=0),
+    )
+    input_recv, others = settle(input_recv, others)
+    short_iso, short_trans, long_iso, long_trans, merge_total, ff_in_total, ff_out_total = others
+    return (
+        out[None],
+        loss,
+        (input_own.astype(F32) + input_recv.astype(F32))[None],
+        placed(grad_down, down_recv, 0, plan.down_rows[0]),
+        short_iso,
+        short_trans,
+        placed(grad_down, down_recv, 1, plan.down_rows[1]),
+        long_iso,
+        long_trans,
+        bias_total,
+        branch_total[:, 2],
+        merge_total,
+        small[0:4],
+        small[4:6],
+        ff_in_total,
+        small[6 : 6 + ff_parts].reshape(-1),
+        ff_out_total,
     )
 
 
@@ -175,7 +1351,7 @@
     return (delta_series, padded_grads, vectors, gain_inner + gain_outer)
 
 
-def body(
+def plain_body(
     series_in,
     target,
     horizons,
@@ -374,28 +1550,43 @@
         P(),
         P(),
     )
-    return jax.shard_map(
-        body,
-        mesh=mesh,
-        in_specs=placed,
-        out_specs=(
-            P("series", "branch", None),
-            P("series"),
-            P("series", None, None),
-            P("series", None),
-            P("series", None),
-            P("series", None),
-            P("series", None),
-            P("series", None),
-            P("series", None),
-            P(),
-            P(),
-            P(),
-            P(),
-            P(),
-            P(None, "series"),
-            P(),
-            P("series", None),
-        ),
-        check_vma=False,
-    )
+
+    def run(*args):
+        shards = mesh.shape["series"]
+        features = args[0].shape[2]
+        down_rows = [args[i].shape[0] // shards for i in (4, 7)]
+        iso_rows = [args[i].shape[0] // shards for i in (5, 8)]
+        fits = (
+            args[0].shape[0] == shards
+            and shards == 16
+            and shards & (shards - 1) == 0
+            and all(r % LANE == 0 and r <= features and 4 * r % features == 0 for r in down_rows)
+            and all(r % 16 == 0 for r in iso_rows)
+        )
+        return jax.shard_map(
+            body if fits else plain_body,
+            mesh=mesh,
+            in_specs=placed,
+            out_specs=(
+                P("series", "branch", None),
+                P("series"),
+                P("series", None, None),
+                P("series", None),
+                P("series", None),
+                P("series", None),
+                P("series", None),
+                P("series", None),
+                P("series", None),
+                P(),
+                P(),
+                P(),
+                P(),
+                P(),
+                P(None, "series"),
+                P(),
+                P("series", None),
+            ),
+            check_vma=False,
+        )(*args)
+
+    return run

time: 2380 us -> 403 us (0.17)
  waiting for transfers between devices: 1610 us -> 154 us
  local copies, waits for them, and re-layouts: 342 us -> 30.4 us
  other arithmetic: 176 us -> 24 us
  matrix products: 145 us -> 0 us
  starting transfers between devices: 4.73 us -> 89.8 us
  Pallas kernels: 0 us -> 78.7 us
  blocking collectives: 60.6 us -> 0 us
    reduce_scatter x5 -> x0, waiting for transfers between devices: 1030 us -> none  [the longest x1 678 us: body(): lax.psum_scatter(padded_grads[1], 'series', scatter_dimension=0, tiled=True)]
    all_gather x3 -> x1, waiting for transfers between devices: 329 us -> 3.12 us  [body(): merge_all = lax.all_gather(merge_own.astype(BF), 'series', axis=0)]
    psum x2 -> x0, waiting for transfers between devices: 239 us -> none  [the longest x1 125 us: body(): lax.psum((grad_merge, head_vectors, head_gains, ff_bias_grad, full_bias,...]
    ppermute x0 -> x79, waiting for transfers between devices: none -> 151 us  [the longest x69 119 us: hop(): lax.ppermute(values, 'series', [(i, i ^ distance) for i in range(shards)])]
    dot_general x21 -> x0, matrix products: 145 us -> none  [the longest x7 51.4 us: product(): jnp.dot(first_operand, second_operand, preferred_element_type=jnp.float32)]
    scatter-add x68 -> x0, local copies, waits for them, and re-layouts: 106 us -> none  [branch_back(): delta_padded.at[:, offset:offset + step_count]]
    add x70 -> x9, other arithmetic: 105 us -> 8.17 us  [the longest x2 2.89 us: scatter_sum(): first = keep + hop(send, 1, shards).astype(F32)]
    ppermute x0 -> x79, starting transfers between devices: none -> 89.8 us  [the longest x69 82.4 us: hop(): lax.ppermute(values, 'series', [(i, i ^ distance) for i in range(shards)])]
  transfers between devices with their start and end apart: 11 -> 80, of which waited for: 9 -> 44; matrix products, arithmetic and copies ran while one was open for 22% -> 7% of each run, Pallas kernels for 0% -> 10%
where the time goes in v2:
time: 403 us; the launch traced here: 395 us
  waiting for transfers between devices  154 us (38%)
  starting transfers between devices  89.8 us (22%)
  Pallas kernels  78.7 us (20%)
  local copies, waits for them, and re-layouts  30.4 us (8%)
  other arithmetic  24 us (6%)
  between operations  17.9 us (4%)
    ppermute x69, waiting for transfers between devices, hop(): lax.ppermute(values, 'series', [(i, i ^ distance) for i in range(shards)])  119 us
    ppermute x69, starting transfers between devices, hop(): lax.ppermute(values, 'series', [(i, i ^ distance) for i in range(shards)])  82.4 us
    ppermute x10, waiting for transfers between devices, swap(): return lax.ppermute(values, 'branch', [(0, 1), (1, 0)])  31.9 us
    unnamed x178, local copies, waits for them, and re-layouts  22.2 us
    pallas_call x2, Pallas kernels, iso_weight(): call(kernel, [SMEM] + vmem(8), [((own, features), F32), ((1, features), F...  20.6 us
    pallas_call x2, Pallas kernels, iso_partial(): call(kernel, [SMEM] + vmem(2) + [HBM] * 2, [((half, rows, features), F32)...  18.4 us
    pallas_call x1, Pallas kernels, head_rows(): call(kernel, [SMEM] + vmem(8) + [HBM] * 2, [(dims, BF), (dims, BF), (dims...  11 us
  transfers between devices with their start and end apart: 80, of which 44 were waited for; matrix products, arithmetic and copies ran while one was open for 7% of the time, Pallas kernels for 10%

profile of v2, /device:TPU:0, one launch (start us, length us, event | category | flops | bytes accessed | tf_op | source)
XLA Modules:
  0.0 394.8 jit_solution(2964678166652533940)
XLA Ops:
  18.3 6.0 %collective-permute-done.refs_1_ = bf16[832,128]{1,0:T(8,128)(2,1)S(1)} collective-permute-done((bf16[832,128]{1,0:T(8,128)(2,1)S(1)}, bf16[832,128]{1,0:T(8,128)(2,1)S(1)}, u32[]{:S(2)}, u32[]{:S(2)}) %collective-permute-start) | collective-permute-done | bytes 213024 | tf_op jit(solution)/shard_map/ppermute | solution.py:936
  24.2 9.4 %collective-permute-done.1.refs_2_ = bf16[832,128]{1,0:T(8,128)(2,1)S(1)} collective-permute-done((bf16[832,128]{1,0:T(8,128)(2,1)S(1)}, bf16[832,128]{1,0:T(8,128)(2,1)S(1)}, u32[]{:S(2)}, u32[]{:S(2)}) %collective-permute-start.1) | collective-permute-done | bytes 213024 | tf_op jit(solution)/shard_map/ppermute | solution.py:936
  38.2 3.4 collective-permute-start.6
  44.8 5.7 %collective-permute-done.7.refs_2_ = bf16[72,512]{1,0:T(8,128)(2,1)S(1)} collective-permute-done((bf16[72,512]{1,0:T(8,128)(2,1)S(1)}, bf16[72,512]{1,0:T(8,128)(2,1)S(1)}, u32[]{:S(2)}, u32[]{:S(2)}) %collective-permute-start.7) | collective-permute-done | bytes 73760 | tf_op jit(solution)/shard_map/ppermute | solution.py:936
  71.0 9.2 %shard_map.308 = (f32[8,72,512]{2,1,0:T(8,128)}, bf16[8,72,512]{2,1,0:T(8,128)(2,1)}) custom-call(s32[8]{0:T(128)} %copy-done.23, bf16[8,72,512]{2,1,0:T(8,128)(2,1)} %copy-done.37, bf16[8,72,512]{2,1,0:T(8,128)(2,1)} %copy-done.44, bf16[2208,512]{1,0:T(8,128)(2,1)} %ws_ref.3, bf16[1664,512]{1,0:T(8,128)(2,1)} %wl_ref.3), custom_call_target="tpu_custom_call" | custom-call | flops 3623878656 | bytes 10485760 | tf_op jit(solution)/shard_map/pallas_call | solution.py:338
  85.4 7.7 %collective-permute-done.21 = bf16[4,72,512]{2,1,0:T(8,128)(2,1)S(1)} collective-permute-done((bf16[4,72,512]{2,1,0:T(8,128)(2,1)S(1)}, bf16[4,72,512]{2,1,0:T(8,128)(2,1)S(1)}, u32[]{:S(2)}, u32[]{:S(2)}) %collective-permute-start.21) | collective-permute-done | bytes 294944 | tf_op jit(solution)/shard_map/ppermute | solution.py:936
  122.2 6.2 %collective-permute-done.29.refs_1_ = bf16[832,128]{1,0:T(8,128)(2,1)S(1)} collective-permute-done((bf16[832,128]{1,0:T(8,128)(2,1)S(1)}, bf16[832,128]{1,0:T(8,128)(2,1)S(1)}, u32[]{:S(2)}, u32[]{:S(2)}) %collective-permute-start.29) | collective-permute-done | bytes 213024 | tf_op jit(solution)/shard_map/ppermute | solution.py:936
  128.3 6.6 %collective-permute-done.30.refs_2_ = bf16[832,128]{1,0:T(8,128)(2,1)S(1)} collective-permute-done((bf16[832,128]{1,0:T(8,128)(2,1)S(1)}, bf16[832,128]{1,0:T(8,128)(2,1)S(1)}, u32[]{:S(2)}, u32[]{:S(2)}) %collective-permute-start.30) | collective-permute-done | bytes 213024 | tf_op jit(solution)/shard_map/ppermute | solution.py:936
  144.2 8.6 %collective-permute-done.34.recv_ref = bf16[408,512]{1,0:T(8,128)(2,1)} collective-permute-done((bf16[408,512]{1,0:T(8,128)(2,1)}, bf16[408,512]{1,0:T(8,128)(2,1)}, u32[]{:S(2)}, u32[]{:S(2)}) %collective-permute-start.34) | collective-permute-done | bytes 417824 | tf_op jit(solution)/shard_map/ppermute | solution.py:940
  152.9 11.0 %shard_map.312 = (bf16[408,512]{1,0:T(8,128)(2,1)}, bf16[408,512]{1,0:T(8,128)(2,1)}, bf16[408,512]{1,0:T(8,128)(2,1)}, bf16[408,512]{1,0:T(8,128)(2,1)}, bf16[4...) custom-call(s32[8]{0:T(128)} %copy-done.23, ...), custom_call_target="tpu_custom_call" | custom-call | flops 4278190080 | bytes 14680064 | tf_op jit(solution)/shard_map/pallas_call | solution.py:866
  170.1 4.5 %shard_map.316 = (bf16[2,8,160,512]{3,2,1,0:T(8,128)(2,1)S(1)}, bf16[2,8,160,512]{3,2,1,0:T(8,128)(2,1)S(1)}) custom-call(s32[8]{0:T(128)S(1)} %copy-done.25, bf16[408,512]{1,0:T(8,128)(2,1)S(1)} %copy-done.55, bf16[408,512]{1,0:T(8,128)(2,1)} %collective-permute-done.34.recv_ref, bf16[408,512]{1,0:T(8,128)(2,1)S(1)} %copy-done.59, ...), custom_call_target="tpu_custom_call" | custom-call | flops 1711276032 | bytes 12582912 | tf_op jit(solution)/shard_map/pallas_call | solution.py:920
  179.2 4.9 %collective-permute-done.44 = bf16[2,8,160,512]{3,2,1,0:T(8,128)(2,1)S(1)} collective-permute-done((bf16[2,8,160,512]{3,2,1,0:T(8,128)(2,1)S(1)}, bf16[2,8,160,512]{3,2,1,0:T(8,128)(2,1)S(1)}, u32[]{:S(2)}, u32[]{:S(2)}) %collective-permute-start.44) | collective-permute-done | bytes 2621472 | tf_op jit(solution)/shard_map/ppermute | solution.py:936
  185.8 5.2 %collective-permute-start.38 = (bf16[832,128]{1,0:T(8,128)(2,1)S(1)}, bf16[832,128]{1,0:T(8,128)(2,1)S(1)}, u32[]{:S(2)}, u32[]{:S(2)}) collective-permute-start(bf16[832,128]{1,0:T(8,128)(2,1)S(1)} %get-tuple-element.366), channel_id=1, source_target_pairs={{0,4},{1,5},{2,6},{3,7},{4,0},{5,1},{6,2},{7,3},{8,12},{9,13},{10,... | collective-permute-start | bytes 638984 | tf_op jit(solution)/shard_map/ppermute | solution.py:936
  193.5 6.5 %collective-permute-done.38.refs_1_ = bf16[832,128]{1,0:T(8,128)(2,1)S(1)} collective-permute-done((bf16[832,128]{1,0:T(8,128)(2,1)S(1)}, bf16[832,128]{1,0:T(8,128)(2,1)S(1)}, u32[]{:S(2)}, u32[]{:S(2)}) %collective-permute-start.38) | collective-permute-done | bytes 213024 | tf_op jit(solution)/shard_map/ppermute | solution.py:936
  200.0 9.2 %collective-permute-done.39.refs_2_ = bf16[832,128]{1,0:T(8,128)(2,1)S(1)} collective-permute-done((bf16[832,128]{1,0:T(8,128)(2,1)S(1)}, bf16[832,128]{1,0:T(8,128)(2,1)S(1)}, u32[]{:S(2)}, u32[]{:S(2)}) %collective-permute-start.39) | collective-permute-done | bytes 213024 | tf_op jit(solution)/shard_map/ppermute | solution.py:936
  211.8 3.8 collective-permute-start.41
  230.2 4.2 %collective-permute-done.47 = bf16[72,512]{1,0:T(8,128)(2,1)S(1)} collective-permute-done((bf16[72,512]{1,0:T(8,128)(2,1)S(1)}, bf16[72,512]{1,0:T(8,128)(2,1)S(1)}, u32[]{:S(2)}, u32[]{:S(2)}) %collective-permute-start.47) | collective-permute-done | bytes 73760 | tf_op jit(solution)/shard_map/ppermute | solution.py:936
  246.9 9.2 %shard_map.318 = (f32[8,72,512]{2,1,0:T(8,128)}, bf16[8,72,512]{2,1,0:T(8,128)(2,1)}) custom-call(s32[8]{0:T(128)} %copy-done.23, bf16[8,72,512]{2,1,0:T(8,128)(2,1)} %copy-done.41, bf16[8,72,512]{2,1,0:T(8,128)(2,1)} %copy-done.47, bf16[2208,512]{1,0:T(8,128)(2,1)} %ws_ref.3, bf16[1664,512]{1,0:T(8,128)(2,1)} %wl_ref.3), custom_call_target="tpu_custom_call" | custom-call | flops 3623878656 | bytes 10485760 | tf_op jit(solution)/shard_map/pallas_call | solution.py:338
  271.5 10.6 %collective-permute-done.59 = bf16[2,160,512]{2,1,0:T(8,128)(2,1)} collective-permute-done((bf16[2,160,512]{2,1,0:T(8,128)(2,1)S(1)}, bf16[2,160,512]{2,1,0:T(8,128)(2,1)}, u32[]{:S(2)}, u32[]{:S(2)}) %collective-permute-start.59) | collective-permute-done | bytes 327712 | tf_op jit(solution)/shard_map/ppermute | solution.py:936
  288.2 3.4 collective-permute-done.61.refs_2_
  299.6 11.3 %shard_map.320 = (f32[2208,512]{1,0:T(8,128)}, f32[1,512]{1,0:T(1,128)S(1)}) custom-call(s32[8]{0:T(128)S(1)} %copy-done.26, bf16[8,72,512]{2,1,0:T(8,128)(2,1)S(1)} %copy-done.39, bf16[8,72,512]{2,1,0:T(8,128)(2,1)S(1)} %copy-done.45, bf16[8,72,512]{2,1,0:T(8,128)(2,1)} %collective-permute-done.33.refs_2_, ...), custom_call_target="tpu_custom_call" | custom-call | flops 3623878656 | bytes 10485760 | tf_op jit(solution)/shard_map/pallas_call | solution.py:385
  321.5 5.4 %collective-permute-done.73 = bf16[160,512]{1,0:T(8,128)(2,1)S(1)} collective-permute-done((bf16[160,512]{1,0:T(8,128)(2,1)S(1)}, bf16[160,512]{1,0:T(8,128)(2,1)S(1)}, u32[]{:S(2)}, u32[]{:S(2)}) %collective-permute-start.73) | collective-permute-done | bytes 163872 | tf_op jit(solution)/shard_map/ppermute | solution.py:940
  347.5 9.3 %shard_map.324 = (f32[1664,512]{1,0:T(8,128)}, f32[1,512]{1,0:T(1,128)S(1)}) custom-call(s32[8]{0:T(128)S(1)} %copy-done.26, bf16[8,72,512]{2,1,0:T(8,128)(2,1)S(1)} %copy-done.40, bf16[8,72,512]{2,1,0:T(8,128)(2,1)S(1)} %copy-done.46, bf16[8,72,512]{2,1,0:T(8,128)(2,1)} %collective-permute-done.33.refs_2_, ...), custom_call_target="tpu_custom_call" | custom-call | flops 2415919104 | bytes 10485760 | tf_op jit(solution)/shard_map/pallas_call | solution.py:385
  359.1 11.8 %collective-permute-done.76 = f32[18,512]{1,0:T(8,128)S(1)} collective-permute-done((f32[18,512]{1,0:T(8,128)S(1)}, f32[18,512]{1,0:T(8,128)S(1)}, u32[]{:S(2)}, u32[]{:S(2)}) %collective-permute-start.76) | collective-permute-done | bytes 36896 | tf_op jit(solution)/shard_map/ppermute | solution.py:940
  (406 shorter events, 203.7 us)
Async XLA Ops:
  7.2 373.2 %all-gather.2.cloned.1.call-start = ((), (), s32[]{:S(2)}) async-start(), calls=%async_computation | async-start | bytes 1114112 | tf_op jit(solution)/shard_map/all_gather | solution.py:1151
  10.7 23.0 %collective-permute-start.4 = (bf16[512,512]{1,0:T(8,128)(2,1)S(1)}, bf16[512,512]{1,0:T(8,128)(2,1)S(1)}, u32[]{:S(2)}, u32[]{:S(2)}) collective-permute-start(bf16[512,512]{1,0:T(8,128)(2,1)S(1)} %pad_select_fusion.1.refs_4_), channel_id=1, source_target_pairs={{0,2},{1,3},{2,0},{3,1},{4,6},{5,7},{6,4},{7,5},{8,10},{9,11},{10,... | collective-permute-start | bytes 1572872 | tf_op jit(solution)/shard_map/ppermute | solution.py:936
  15.4 18.2 %collective-permute-start.1 = (bf16[832,128]{1,0:T(8,128)(2,1)S(1)}, bf16[832,128]{1,0:T(8,128)(2,1)S(1)}, u32[]{:S(2)}, u32[]{:S(2)}) collective-permute-start(bf16[832,128]{1,0:T(8,128)(2,1)S(1)} %get-tuple-element.373), channel_id=1, source_target_pairs={{0,8},{1,9},{2,10},{3,11},{4,12},{5,13},{6,14},{7,15},{8,0},{9,1},... | collective-permute-start | bytes 638984 | tf_op jit(solution)/shard_map/ppermute | solution.py:936
  18.0 15.6 %collective-permute-start.2 = (bf16[832,128]{1,0:T(8,128)(2,1)S(1)}, bf16[832,128]{1,0:T(8,128)(2,1)S(1)}, u32[]{:S(2)}, u32[]{:S(2)}) collective-permute-start(bf16[832,128]{1,0:T(8,128)(2,1)S(1)} %get-tuple-element.372), channel_id=1, source_target_pairs={{0,12},{1,13},{2,14},{3,15},{4,8},{5,9},{6,10},{7,11},{8,4},{9,5},... | collective-permute-start | bytes 638984 | tf_op jit(solution)/shard_map/ppermute | solution.py:936
  18.3 15.5 %collective-permute-start.3 = (bf16[512,512]{1,0:T(8,128)(2,1)S(1)}, bf16[512,512]{1,0:T(8,128)(2,1)S(1)}, u32[]{:S(2)}, u32[]{:S(2)}) collective-permute-start(bf16[512,512]{1,0:T(8,128)(2,1)S(1)} %pad_select_fusion.1.refs_4_), channel_id=1, source_target_pairs={{0,1},{1,0},{2,3},{3,2},{4,5},{5,4},{6,7},{7,6},{8,9},{9,8},{10,11... | collective-permute-start | bytes 1572872 | tf_op jit(solution)/shard_map/ppermute | solution.py:936
  44.3 22.8 %collective-permute-start.18 = (bf16[512,512]{1,0:T(8,128)(2,1)S(1)}, bf16[512,512]{1,0:T(8,128)(2,1)S(1)}, u32[]{:S(2)}, u32[]{:S(2)}) collective-permute-start(bf16[512,512]{1,0:T(8,128)(2,1)S(1)} %pad_select_fusion.refs_4_), channel_id=1, source_target_pairs={{0,2},{1,3},{2,0},{3,1},{4,6},{5,7},{6,4},{7,5},{8,10},{9,11},{10,... | collective-permute-start | bytes 1572872 | tf_op jit(solution)/shard_map/ppermute | solution.py:936
  115.8 19.1 %collective-permute-start.32 = (bf16[288,512]{1,0:T(8,128)(2,1)S(1)}, bf16[288,512]{1,0:T(8,128)(2,1)S(1)}, u32[]{:S(2)}, u32[]{:S(2)}) collective-permute-start(bf16[288,512]{1,0:T(8,128)(2,1)S(1)} %get-tuple-element.190), channel_id=1, source_target_pairs={{0,3},{1,2},{2,1},{3,0},{4,7},{5,6},{6,5},{7,4},{8,11},{9,10},{10,... | collective-permute-start | bytes 884744 | tf_op jit(solution)/shard_map/ppermute | solution.py:936
  116.8 18.1 %collective-permute-start.30 = (bf16[832,128]{1,0:T(8,128)(2,1)S(1)}, bf16[832,128]{1,0:T(8,128)(2,1)S(1)}, u32[]{:S(2)}, u32[]{:S(2)}) collective-permute-start(bf16[832,128]{1,0:T(8,128)(2,1)S(1)} %get-tuple-element.369), channel_id=1, source_target_pairs={{0,8},{1,9},{2,10},{3,11},{4,12},{5,13},{6,14},{7,15},{8,0},{9,1},... | collective-permute-start | bytes 638984 | tf_op jit(solution)/shard_map/ppermute | solution.py:936
  118.8 16.1 %collective-permute-start.31 = (bf16[832,128]{1,0:T(8,128)(2,1)S(1)}, bf16[832,128]{1,0:T(8,128)(2,1)S(1)}, u32[]{:S(2)}, u32[]{:S(2)}) collective-permute-start(bf16[832,128]{1,0:T(8,128)(2,1)S(1)} %get-tuple-element.368), channel_id=1, source_target_pairs={{0,12},{1,13},{2,14},{3,15},{4,8},{5,9},{6,10},{7,11},{8,4},{9,5},... | collective-permute-start | bytes 638984 | tf_op jit(solution)/shard_map/ppermute | solution.py:936
  185.2 37.8 %collective-permute-start.45 = (bf16[2,4,160,512]{3,2,1,0:T(8,128)(2,1)S(1)}, bf16[2,4,160,512]{3,2,1,0:T(8,128)(2,1)S(1)}, u32[]{:S(2)}, u32[]{:S(2)}) collective-permute-start(bf16[2,4,160,512]{3,2,1,0:T(8,128)(2,1)S(1)} %slice.404), channel_id=1, source_target_pairs={{0,2},{1,3},{2,0},{3,1},{4,6},{5,7},{6,4},{7,5},{8,10},{9,11},{10,... | collective-permute-start | bytes 3932168 | tf_op jit(solution)/shard_map/ppermute | solution.py:936
  191.1 18.2 %collective-permute-start.39 = (bf16[832,128]{1,0:T(8,128)(2,1)S(1)}, bf16[832,128]{1,0:T(8,128)(2,1)S(1)}, u32[]{:S(2)}, u32[]{:S(2)}) collective-permute-start(bf16[832,128]{1,0:T(8,128)(2,1)S(1)} %get-tuple-element.365), channel_id=1, source_target_pairs={{0,8},{1,9},{2,10},{3,11},{4,12},{5,13},{6,14},{7,15},{8,0},{9,1},... | collective-permute-start | bytes 638984 | tf_op jit(solution)/shard_map/ppermute | solution.py:936
  192.0 17.3 %collective-permute-start.40 = (bf16[832,128]{1,0:T(8,128)(2,1)S(1)}, bf16[832,128]{1,0:T(8,128)(2,1)S(1)}, u32[]{:S(2)}, u32[]{:S(2)}) collective-permute-start(bf16[832,128]{1,0:T(8,128)(2,1)S(1)} %get-tuple-element.364), channel_id=1, source_target_pairs={{0,12},{1,13},{2,14},{3,15},{4,8},{5,9},{6,10},{7,11},{8,4},{9,5},... | collective-permute-start | bytes 638984 | tf_op jit(solution)/shard_map/ppermute | solution.py:936
  228.8 16.4 %collective-permute-start.55 = (bf16[4,160,512]{2,1,0:T(8,128)(2,1)S(1)}, bf16[4,160,512]{2,1,0:T(8,128)(2,1)S(1)}, u32[]{:S(2)}, u32[]{:S(2)}) collective-permute-start(bf16[4,160,512]{2,1,0:T(8,128)(2,1)S(1)} %fusion.3), channel_id=1, source_target_pairs={{0,16},{16,0},{1,17},{17,1},{2,18},{18,2},{3,19},{19,3},{4,20},{20... | collective-permute-start | bytes 1966088 | tf_op jit(solution)/shard_map/ppermute | solution.py:940
  256.1 25.9 %collective-permute-start.58 = (bf16[8,72,512]{2,1,0:T(8,128)(2,1)}, bf16[8,72,512]{2,1,0:T(8,128)(2,1)S(1)}, u32[]{:S(2)}, u32[]{:S(2)}) collective-permute-start(bf16[8,72,512]{2,1,0:T(8,128)(2,1)} %copy-done.41), channel_id=1, source_target_pairs={{0,16},{16,0},{1,17},{17,1},{2,18},{18,2},{3,19},{19,3},{4,20},{20... | collective-permute-start | bytes 1769480 | tf_op jit(solution)/shard_map/ppermute | solution.py:940
  264.5 17.6 %collective-permute-start.59 = (bf16[2,160,512]{2,1,0:T(8,128)(2,1)S(1)}, bf16[2,160,512]{2,1,0:T(8,128)(2,1)}, u32[]{:S(2)}, u32[]{:S(2)}) collective-permute-start(bf16[2,160,512]{2,1,0:T(8,128)(2,1)S(1)} %slice.405), channel_id=1, source_target_pairs={{0,8},{1,9},{2,10},{3,11},{4,12},{5,13},{6,14},{7,15},{8,0},{9,1},... | collective-permute-start | bytes 983048 | tf_op jit(solution)/shard_map/ppermute | solution.py:936
  292.2 18.7 %collective-permute-start.67 = (bf16[512,512]{1,0:T(8,128)(2,1)}, bf16[512,512]{1,0:T(8,128)(2,1)S(1)}, u32[]{:S(2)}, u32[]{:S(2)}) collective-permute-start(bf16[512,512]{1,0:T(8,128)(2,1)} %fusion.4), channel_id=1, source_target_pairs={{0,2},{1,3},{2,0},{3,1},{4,6},{5,7},{6,4},{7,5},{8,10},{9,11},{10,... | collective-permute-start | bytes 1572872 | tf_op jit(solution)/shard_map/ppermute | solution.py:936
  294.3 16.7 %collective-permute-start.64 = (bf16[112,512]{1,0:T(8,128)(2,1)S(1)}, bf16[112,512]{1,0:T(8,128)(2,1)S(1)}, u32[]{:S(2)}, u32[]{:S(2)}) collective-permute-start(bf16[112,512]{1,0:T(8,128)(2,1)S(1)} %shard_map.319.refs_0_), channel_id=1, source_target_pairs={{0,4},{1,5},{2,6},{3,7},{4,0},{5,1},{6,2},{7,3},{8,12},{9,13},{10,... | collective-permute-start | bytes 344072 | tf_op jit(solution)/shard_map/ppermute | solution.py:936
  296.1 14.9 %collective-permute-start.65 = (bf16[112,512]{1,0:T(8,128)(2,1)S(1)}, bf16[112,512]{1,0:T(8,128)(2,1)S(1)}, u32[]{:S(2)}, u32[]{:S(2)}) collective-permute-start(bf16[112,512]{1,0:T(8,128)(2,1)S(1)} %shard_map.319.refs_0_), channel_id=1, source_target_pairs={{0,8},{1,9},{2,10},{3,11},{4,12},{5,13},{6,14},{7,15},{8,0},{9,1},... | collective-permute-start | bytes 344072 | tf_op jit(solution)/shard_map/ppermute | solution.py:936
  311.2 23.5 %collective-permute-start.74 = (bf16[512,512]{1,0:T(8,128)(2,1)S(1)}, bf16[512,512]{1,0:T(8,128)(2,1)S(1)}, u32[]{:S(2)}, u32[]{:S(2)}) collective-permute-start(bf16[512,512]{1,0:T(8,128)(2,1)S(1)} %fusion.2), channel_id=1, source_target_pairs={{0,16},{16,0},{1,17},{17,1},{2,18},{18,2},{3,19},{19,3},{4,20},{20... | collective-permute-start | bytes 1572872 | tf_op jit(solution)/shard_map/ppermute | solution.py:940
  311.3 15.6 %collective-permute-start.73 = (bf16[160,512]{1,0:T(8,128)(2,1)S(1)}, bf16[160,512]{1,0:T(8,128)(2,1)S(1)}, u32[]{:S(2)}, u32[]{:S(2)}) collective-permute-start(bf16[160,512]{1,0:T(8,128)(2,1)S(1)} %fusion.11), channel_id=1, source_target_pairs={{0,16},{16,0},{1,17},{17,1},{2,18},{18,2},{3,19},{19,3},{4,20},{20... | collective-permute-start | bytes 491528 | tf_op jit(solution)/shard_map/ppermute | solution.py:940
  316.4 18.3 %collective-permute-start.72 = (bf16[4,112,512]{2,1,0:T(8,128)(2,1)S(1)}, bf16[4,112,512]{2,1,0:T(8,128)(2,1)S(1)}, u32[]{:S(2)}, u32[]{:S(2)}) collective-permute-start(bf16[4,112,512]{2,1,0:T(8,128)(2,1)S(1)} %pad_maximum_fusion), channel_id=1, source_target_pairs={{0,2},{1,3},{2,0},{3,1},{4,6},{5,7},{6,4},{7,5},{8,10},{9,11},{10,... | collective-permute-start | bytes 1376264 | tf_op jit(solution)/shard_map/ppermute | solution.py:936
  337.6 21.6 %collective-permute-start.77 = (bf16[816,512]{1,0:T(8,128)(2,1)S(1)}, bf16[816,512]{1,0:T(8,128)(2,1)}, u32[]{:S(2)}, u32[]{:S(2)}) collective-permute-start(bf16[816,512]{1,0:T(8,128)(2,1)S(1)} %shard_map.322), channel_id=1, source_target_pairs={{0,16},{16,0},{1,17},{17,1},{2,18},{18,2},{3,19},{19,3},{4,20},{20... | collective-permute-start | bytes 2506760 | tf_op jit(solution)/shard_map/ppermute | solution.py:940
  345.3 29.9 %collective-permute-start.78 = (bf16[512,512]{1,0:T(8,128)(2,1)S(1)}, bf16[512,512]{1,0:T(8,128)(2,1)S(1)}, u32[]{:S(2)}, u32[]{:S(2)}) collective-permute-start(bf16[512,512]{1,0:T(8,128)(2,1)S(1)} %get-tuple-element.287), channel_id=1, source_target_pairs={{0,16},{16,0},{1,17},{17,1},{2,18},{18,2},{3,19},{19,3},{4,20},{20... | collective-permute-start | bytes 1572872 | tf_op jit(solution)/shard_map/ppermute | solution.py:940
  346.6 24.3 %collective-permute-start.76 = (f32[18,512]{1,0:T(8,128)S(1)}, f32[18,512]{1,0:T(8,128)S(1)}, u32[]{:S(2)}, u32[]{:S(2)}) collective-permute-start(f32[18,512]{1,0:T(8,128)S(1)} %maximum_maximum_fusion), channel_id=1, source_target_pairs={{0,16},{16,0},{1,17},{17,1},{2,18},{18,2},{3,19},{19,3},{4,20},{20... | collective-permute-start | bytes 110600 | tf_op jit(solution)/shard_map/ppermute | solution.py:940
  (134 other events, 1459.7 us)
Sparse Core Ops, SparseCore 0:
  341.2 39.0 all-gather.1
